TPU v7x, 32 devices: a whole 2x2x4 slice. The times are simulated.
32 devices in a mesh: region: 8 (over y, x, core), sub: 4 (over z).
Axes of the slice: x: 2, y: 2, z: 4, core: 2. Of those that a mesh axis runs over, the one named last changes fastest.
Arguments:
- state_anom: bfloat16 [64, 64, 4096], P(('region', 'sub')), may hold values from -6 to 6
- obs_anom: bfloat16 [768, 64, 128], P(('region', 'sub')), may hold values from -6 to 6
- innovations: bfloat16 [768, 128], P(('region', 'sub')), may hold values from -6 to 6
- obs_error: bfloat16 [768, 128], P(('region', 'sub')), may hold values from 2 to 16
- influence: int32 [768, 4], P(('region', 'sub')), may hold values from 0 to 63, as said below
- taper_level: int32 [768, 4], P(('region', 'sub')), may hold values from 0 to 3
- obs_count: int32 [8], P('region'), may hold values from 3072 to 12288
Outputs:
- increment: float32 [64, 4096], P(('region', 'sub'))
- variance_drop: float32 [64, 4096], P(('region', 'sub'))
Inputs may be any that keep to these rules, and one draw needn't show every extreme that they name: `influence`: every listed column block lies in the observation block's own region or in a region one index away (regions wrap around). Over the blocks of one device, at most 36 entries name column blocks held by devices of one sub index, and exactly 36 for some sub index.
All inputs are finite; a program needn't handle non-finite values.
Results may differ from a plain program's by a relative error of at most 0.013.
Values may be sent and summed in bfloat16 or wider, within the bound.
No kernel may reach another device: no remote copies, remote signals or barrier semaphores. Data moves between devices by JAX's collectives and lax.ppermute only.
A program may use at most 64 MiB of HBM per device.

v0:
```python
import jax
import jax.numpy as jnp
from jax import lax
from jax.sharding import PartitionSpec as P

HIGHEST = lax.Precision.HIGHEST


def with_halo(shard, sides, width):
    for axis, dim in sides:
        count, length = (lax.axis_size(axis), shard.shape[dim])
        up = [(i, (i + 1) % count) for i in range(count)]
        down = [(j, i) for i, j in up]
        last = lax.slice_in_dim(shard, length - width, length, axis=dim)
        leading = lax.slice_in_dim(shard, 0, width, axis=dim)
        before = lax.ppermute(last, axis, up)
        after = lax.ppermute(leading, axis, down)
        shard = jnp.concatenate([before, shard, after], axis=dim)
    return shard


def block_terms(obs_blocks, innov_blocks, error_blocks, obs_total):
    blocks = obs_blocks.shape[0]
    members = obs_blocks.shape[1]
    per_block = obs_blocks.shape[2]
    divisor = members - 1.0
    spread = (
        jnp.einsum("bmo,bmo->bo", obs_blocks, obs_blocks, preferred_element_type=jnp.float32)
        / divisor
    )
    position = (
        jnp.arange(blocks, dtype=jnp.int32)[:, None] * per_block
        + jnp.arange(per_block, dtype=jnp.int32)[None, :]
    )
    usable = (position < obs_total).astype(jnp.float32)
    factor = usable / (spread + error_blocks.astype(jnp.float32))
    scaled = (obs_blocks.astype(jnp.float32) * (factor / (divisor * divisor))[:, None, :]).astype(
        jnp.bfloat16
    )
    covariance = jnp.einsum("bmo,bno->bmn", scaled, obs_blocks, preferred_element_type=jnp.float32)
    weights = divisor * jnp.einsum(
        "bmo,bo->bm", scaled, innov_blocks, preferred_element_type=jnp.float32
    )
    return jnp.concatenate([weights, covariance.reshape(blocks, members * members)], axis=1)


def locate(targets, region_here, regions, sub_count, col_blocks):
    per_region = sub_count * col_blocks
    target_region = targets // per_region
    target_sub = targets // col_blocks % sub_count
    target_local = targets % col_blocks
    offset = (target_region - region_here + 1 + regions) % regions
    return (target_sub, offset * col_blocks + target_local)


def local(state_anom, obs_anom, innovations, obs_error, influence, taper_level, obs_count):
    sub_count = lax.axis_size("sub")
    regions = lax.axis_size("region")
    sub_here = lax.axis_index("sub")
    region_here = lax.axis_index("region")
    members = obs_anom.shape[1]
    col_blocks = state_anom.shape[0]
    buckets = 3 * col_blocks
    term_width = members * members + members
    obs_total = obs_count[0]
    obs_piece = lax.all_gather(obs_anom, "sub", axis=0, tiled=True)
    innov_piece = lax.all_gather(innovations, "sub", axis=0, tiled=True)
    error_piece = lax.all_gather(obs_error, "sub", axis=0, tiled=True)
    target_piece = lax.all_gather(influence, "sub", axis=0, tiled=True)
    level_piece = lax.all_gather(taper_level, "sub", axis=0, tiled=True)
    partials = block_terms(obs_piece, innov_piece, error_piece, obs_total)
    target_sub, bucket = locate(target_piece, region_here, regions, sub_count, col_blocks)
    tapers = 1.0 - 0.25 * level_piece.astype(jnp.float32)
    matches = (bucket[:, :, None] == jnp.arange(buckets, dtype=jnp.int32)[None, None, :]) & (
        target_sub == sub_here
    )[:, :, None]
    taper_rows = jnp.sum(jnp.where(matches, tapers[:, :, None], 0.0), axis=1)
    totals = jnp.dot(taper_rows.T, partials, precision=HIGHEST, preferred_element_type=jnp.float32)
    layered = totals.reshape(3, col_blocks, term_width)
    padded = with_halo(layered, (("region", 0),), 1)
    merged = padded[2] + padded[0] + padded[4]
    mixer = jnp.concatenate(
        [merged[:, None, :members], merged[:, members:].reshape(col_blocks, members, members)],
        axis=1,
    ).astype(jnp.bfloat16)
    projected = jnp.einsum("kam,kmc->kac", mixer, state_anom, preferred_element_type=jnp.float32)
    increment = projected[:, 0, :]
    variance_drop = jnp.sum(state_anom.astype(jnp.float32) * projected[:, 1:, :], axis=1)
    return (increment, variance_drop)


def solution(mesh):
    return jax.shard_map(
        local,
        mesh=mesh,
        in_specs=(
            P(("region", "sub"), None, None),
            P(("region", "sub"), None, None),
            P(("region", "sub"), None),
            P(("region", "sub"), None),
            P(("region", "sub"), None),
            P(("region", "sub"), None),
            P("region"),
        ),
        out_specs=(P(("region", "sub"), None), P(("region", "sub"), None)),
        check_vma=False,
    )
```

profile of v0, /device:TPU:0, one launch (start us, length us, event | category | flops | bytes accessed | tf_op | source)
XLA Modules:
  0.0 87.7 jit_solution(2662199376395835722)
XLA Ops:
  7.2 0.0 all-gather.4.cloned.1.call-start
  7.2 0.7 all-gather.4.cloned.1.call-update
  8.5 13.7 %all-gather = s32[4,24,4]{1,2,0:T(4,128)S(1)} all-gather(s32[1,24,4]{1,2,0:T(4,128)} %bitcast.34), channel_id=1, replica_groups=mesh['region'=8,'sub'=4] {'sub'}, dimensions={0}, use_global_device_ids=true | all-gather | bytes 1920 | tf_op jit(solution)/shard_map/all_gather | solution.py:69
  22.2 0.1 reshape.28
  22.3 12.3 %all-gather.1 = s32[4,24,4]{1,2,0:T(4,128)S(1)} all-gather(s32[1,24,4]{1,2,0:T(4,128)} %bitcast.35), channel_id=1, replica_groups=mesh['region'=8,'sub'=4] {'sub'}, dimensions={0}, use_global_device_ids=true | all-gather | bytes 1920 | tf_op jit(solution)/shard_map/all_gather | solution.py:70
  34.7 0.1 reshape.35
  34.7 13.4 %all_gather.19 = bf16[96,128]{1,0:T(8,128)(2,1)S(1)} all-gather(bf16[24,128]{1,0:T(8,128)(2,1)} %param.9), channel_id=1, replica_groups=mesh['region'=8,'sub'=4] {'sub'}, dimensions={0}, use_global_device_ids=true | all-gather | bytes 30720 | tf_op jit(solution)/shard_map/all_gather | solution.py:67
  48.2 13.3 %all_gather.18 = bf16[96,128]{1,0:T(8,128)(2,1)S(1)} all-gather(bf16[24,128]{1,0:T(8,128)(2,1)} %param.10), channel_id=1, replica_groups=mesh['region'=8,'sub'=4] {'sub'}, dimensions={0}, use_global_device_ids=true | all-gather | bytes 30720 | tf_op jit(solution)/shard_map/all_gather | solution.py:68
  61.6 0.0 all-gather.4.cloned.1.call-done
  61.6 0.0 copy-start
  61.6 2.1 %fusion = f32[96,128]{1,0:T(8,128)S(1)} fusion(bf16[96,64,128]{2,1,0:T(8,128)(2,1)} %all-gather.4.cloned.1.call-done), kind=kLoop, calls=%fused_computation.1 | loop fusion | flops 2347008 | bytes 1622016 | tf_op jit(solution)/shard_map/bmo,bmo->bo/dot_general | solution.py:28
  63.7 0.1 divide_multiply_fusion
  63.8 2.3 %fusion.2 = f32[96,1,64]{2,1,0:T(1,128)S(1)} fusion(bf16[96,64,128]{2,1,0:T(8,128)(2,1)} %all-gather.4.cloned.1.call-done, f32[96,128]{1,0:T(8,128)S(1)} %divide_multiply_fusion, bf16[96,128,1]{1,0,2:T(8,128)(2,1)S(1)} %bitcast.33), kind=kOutput, calls=%fused_computation.4 | convolution fusion | flops 3932160 | bytes 1671168 | tf_op jit(solution)/shard_map/bmo,bo->bm/dot_general | solution.py:41
  66.1 0.1 copy.38
  66.2 0.0 copy-done
  66.2 2.6 %fusion.1 = f32[96,64,64]{2,1,0:T(8,128)} fusion(bf16[96,64,128]{2,1,0:T(8,128)(2,1)S(1)} %copy-done, f32[96,128]{1,0:T(8,128)S(1)} %divide_multiply_fusion), kind=kOutput, calls=%fused_computation.3 | convolution fusion | flops 103022592 | bytes 3194880 | tf_op jit(solution)/shard_map/bmo,bno->bmn/dot_general | solution.py:40
  68.8 3.1 %copy.29 = f32[96,64,64]{0,2,1:T(8,128)S(1)} copy(f32[96,64,64]{2,1,0:T(8,128)} %fusion.1) | data formatting | bytes 3145728 | tf_op jit(solution)/shard_map/bmo,bno->bmn/dot_general | solution.py:40
  71.9 0.0 copy-start.1
  71.9 1.8 %fusion.3 = f32[6,4160]{1,0:T(8,128)S(1)} fusion(f32[96,6]{0,1:T(8,128)S(1)} %select_reduce_fusion, f32[96,4096]{0,1:T(8,128)S(1)} %bitcast.31, f32[96,64]{0,1:T(8,128)S(1)} %bitcast_multiply_fusion), kind=kOutput, calls=%fused_computation.5 | convolution fusion | flops 29153280 | bytes 1699584 | tf_op jit(solution)/shard_map/dot_general | solution.py:78
  73.8 0.1 collective-permute-start
  73.9 2.6 %collective-permute-start.1 = (f32[1,2,4160]{2,1,0:T(2,128)S(1)}, f32[1,2,4160]{2,1,0:T(2,128)S(1)}, u32[]{:S(2)}, u32[]{:S(2)}) collective-permute-start(f32[1,2,4160]{2,1,0:T(2,128)S(1)} %get-tuple-element.3), channel_id=1, source_target_pairs={{4,0},{8,4},{12,8},{16,12},{20,16},{24,20},{28,24},{0,28},{5,1},{9... | collective-permute-start | bytes 99848 | tf_op jit(solution)/shard_map/ppermute | solution.py:17
  76.5 1.6 %collective-permute-done = f32[1,2,4160]{2,1,0:T(2,128)S(1)} collective-permute-done((f32[1,2,4160]{2,1,0:T(2,128)S(1)}, f32[1,2,4160]{2,1,0:T(2,128)S(1)}, u32[]{:S(2)}, u32[]{:S(2)}) %collective-permute-start) | collective-permute-done | bytes 33312 | tf_op jit(solution)/shard_map/ppermute | solution.py:16
  78.1 0.0 collective-permute-done.1
  78.2 0.1 slice.43
  78.2 0.1 reshape.26
  78.3 0.1 copy.31
  78.5 0.1 copy.30
  78.6 0.0 copy-done.1
  78.6 0.6 fusion.13
  79.2 1.1 %fusion.7 = f32[2,4096]{1,0:T(2,128)} fusion(f32[2,65,4096]{2,1,0:T(8,128)S(1)} %fusion.13, bf16[2,64,4096]{2,1,0:T(8,128)(2,1)S(1)} %copy-done.1), kind=kLoop, calls=%fused_computation.10 | loop fusion | flops 1564672 | bytes 3178496 | tf_op jit(solution)/shard_map/reduce_sum | solution.py:88
  80.3 0.6 copy.44
  (12 shorter events, 0.2 us)
Async XLA Ops:
  7.2 54.4 %all-gather.4.cloned.1.call-start = ((), (), s32[]{:S(2)}) async-start(), calls=%async_computation | async-start | bytes 1966080 | tf_op jit(solution)/shard_map/all_gather | solution.py:66
  61.6 4.6 %copy-start = (bf16[96,64,128]{2,1,0:T(8,128)(2,1)S(1)}, bf16[96,64,128]{2,1,0:T(8,128)(2,1)}, u32[]{:S(2)}) copy-start(bf16[96,64,128]{2,1,0:T(8,128)(2,1)} %all-gather.4.cloned.1.call-done) | copy-start | bytes 4718596
  71.9 6.7 %copy-start.1 = (bf16[2,64,4096]{2,1,0:T(8,128)(2,1)S(1)}, bf16[2,64,4096]{2,1,0:T(8,128)(2,1)}, u32[]{:S(2)}) copy-start(bf16[2,64,4096]{2,1,0:T(8,128)(2,1)} %param.7) | copy-start | bytes 3145732
  73.8 4.3 %collective-permute-start = (f32[1,2,4160]{2,1,0:T(2,128)S(1)}, f32[1,2,4160]{2,1,0:T(2,128)S(1)}, u32[]{:S(2)}, u32[]{:S(2)}) collective-permute-start(f32[1,2,4160]{2,1,0:T(2,128)S(1)} %get-tuple-element.2), channel_id=1, source_target_pairs={{0,4},{4,8},{8,12},{12,16},{16,20},{20,24},{24,28},{28,0},{1,5},{5... | collective-permute-start | bytes 99848 | tf_op jit(solution)/shard_map/ppermute | solution.py:16
  73.9 4.2 %collective-permute-start.1 = (f32[1,2,4160]{2,1,0:T(2,128)S(1)}, f32[1,2,4160]{2,1,0:T(2,128)S(1)}, u32[]{:S(2)}, u32[]{:S(2)}) collective-permute-start(f32[1,2,4160]{2,1,0:T(2,128)S(1)} %get-tuple-element.3), channel_id=1, source_target_pairs={{4,0},{8,4},{12,8},{16,12},{20,16},{24,20},{28,24},{0,28},{5,1},{9... | collective-permute-start | bytes 99848 | tf_op jit(solution)/shard_map/ppermute | solution.py:17
Sparse Core Ops, SparseCore 0:
  9.6 40.4 all-gather.3
where the time goes:
time: 88.4 us; the launch traced here: 87.7 us
  blocking collectives  52.8 us (60%)
  between operations  14.8 us (17%)
  matrix products  7.34 us (8%)
  local copies, waits for them, and re-layouts  4.45 us (5%)
  other arithmetic  3.34 us (4%)
  starting transfers between devices  2.73 us (3%)
  waiting for transfers between devices  2.31 us (3%)
    all_gather x1, blocking collectives, local(): target_piece = lax.all_gather(influence, 'sub', axis=0, tiled=True)  13.7 us
    all_gather x1, blocking collectives, local(): innov_piece = lax.all_gather(innovations, 'sub', axis=0, tiled=True)  13.4 us
    all_gather x1, blocking collectives, local(): error_piece = lax.all_gather(obs_error, 'sub', axis=0, tiled=True)  13.3 us
    all_gather x1, blocking collectives, local(): level_piece = lax.all_gather(taper_level, 'sub', axis=0, tiled=True)  12.3 us
    dot_general x1, local copies, waits for them, and re-layouts, block_terms(): jnp.einsum('bmo,bno->bmn', scaled, obs_blocks, preferred_element_type=jnp...  3.08 us
    ppermute x1, starting transfers between devices, with_halo(): after = lax.ppermute(leading, axis, down)  2.63 us
    dot_general x1, matrix products, block_terms(): jnp.einsum('bmo,bno->bmn', scaled, obs_blocks, preferred_element_type=jnp...  2.62 us
    dot_general x1, matrix products, block_terms(): jnp.einsum('bmo,bo->bm', scaled, innov_blocks, preferred_element_type=jnp...  2.33 us
  transfers between devices with their start and end apart: 3, of which 1 were waited for; matrix products, arithmetic and copies ran while one was open for 0% of the time, Pallas kernels for 0%

commit v1 on v0

v1 whole, which is shorter than its diff:
```python
import functools

import jax
import jax.numpy as jnp
from jax import lax
from jax.experimental import pallas as pl
from jax.experimental.pallas import tpu as pltpu
from jax.sharding import PartitionSpec as P

AXES = ("region", "sub")
HALF = 32
SLOT = 48
USED = 40


def lane_patterns(rows):
    row = lax.broadcasted_iota(jnp.int32, (rows, 128), 0)
    lane = lax.broadcasted_iota(jnp.int32, (rows, 128), 1)
    return row, lane, lane % HALF, (lane // HALF) % 2 == 0


def pack_weights(infl_ref, level_ref, rows_ref, weights_ref, group_regions, sub_here, sub_count):
    blocks = infl_ref.shape[1]
    rows_ref[...] = jnp.zeros_like(rows_ref)
    rows_ref[0:4, 0:blocks] = infl_ref[...].astype(jnp.float32)
    rows_ref[4:8, 0:blocks] = 1.0 - 0.25 * level_ref[...].astype(jnp.float32)
    columns = rows_ref[...].T
    targets = [jnp.broadcast_to(columns[0:blocks, n : n + 1], (blocks, 128)) for n in range(4)]
    tapers = [jnp.broadcast_to(columns[0:blocks, 4 + n : 5 + n], (blocks, 128)) for n in range(4)]
    local = lax.broadcasted_iota(jnp.int32, (blocks, 128), 1) // 64
    for g, region in enumerate(group_regions):
        for k, slot in enumerate(slot_order(sub_count)):
            first = (region * sub_count + (sub_here ^ slot)) * 2
            wanted = (first + local).astype(jnp.float32)
            weight = jnp.zeros((blocks, 128), jnp.float32)
            for n in range(4):
                weight = weight + jnp.where(targets[n] == wanted, tapers[n], 0.0)
            weights_ref[g * sub_count + k] = weight


def slot_order(sub_count):
    bits = sub_count.bit_length() - 1
    return sorted(range(sub_count), key=lambda i: [(i >> b) & 1 for b in range(bits)])


def neighbours(regions):
    here = lax.axis_index("region")
    odd = here % 2
    far = (here + 2 * odd - 1 + regions) % regions
    near = here + 1 - 2 * odd
    return here, near, far


def terms_kernel(sub_count, regions, count_ref, infl_ref, level_ref, obs_ref, innov_ref, error_ref,
                 terms_ref, weights_ref, far_ref, rows_ref, error32, innov32):
    blocks, members, per_block = obs_ref.shape
    here, near, far = neighbours(regions)
    sub_here = lax.axis_index("sub")
    divisor = members - 1.0
    error32[...] = error_ref[...].astype(jnp.float32)
    innov32[...] = innov_ref[...].astype(jnp.float32)
    pack_weights(infl_ref, level_ref, rows_ref, weights_ref, (far, near, here), sub_here, sub_count)
    row, lane, column, square = lane_patterns(HALF)
    upper = (row <= column) | ~square
    diagonal = (row == column) & square
    row8 = lax.broadcasted_iota(jnp.int32, (8, 128), 0)
    place = lax.broadcasted_iota(jnp.int32, (1, 128), 1)
    left = count_ref[0] - sub_here * (blocks * per_block)
    for b in range(blocks):
        raw = obs_ref[b]
        values = raw.astype(jnp.float32)
        spread = jnp.sum(values * values, axis=0, keepdims=True) / divisor
        usable = jnp.where(place + b * per_block < left, 1.0 / (divisor * divisor), 0.0)
        factor = usable / (spread + error32[b : b + 1, :])
        scaled = (values * factor).astype(jnp.bfloat16)
        low, high = scaled[:HALF], scaled[HALF:]
        innov = jnp.broadcast_to(innov32[b : b + 1, :], (16, 128)).astype(jnp.bfloat16)
        product = lax.dot_general(
            jnp.concatenate([raw, innov], axis=0),
            jnp.concatenate([low, high, low, high, high, low, high, low], axis=0),
            (((1,), (1,)), ((), ())),
            preferred_element_type=jnp.float32,
        )
        lower = product[HALF : 2 * HALF, 128:]
        terms_ref[b, 0:HALF, :] = jnp.where(upper, product[:HALF, :128], lower)
        corner = jnp.sum(jnp.where(diagonal, lower, 0.0), axis=0, keepdims=True)
        extra = jnp.where(row8 == 0, divisor * product[2 * HALF : 2 * HALF + 8, :128], jnp.where(row8 == 1, corner, 0.0))
        terms_ref[b, HALF:USED, :] = extra
    write_sums(weights_ref, terms_ref, 0, sub_count, far_ref)


def write_sums(weights_ref, terms_ref, first, sub_count, out_ref):
    blocks = terms_ref.shape[0]
    for k in range(0, sub_count, 4):
        count = min(4, sub_count - k)
        totals = [jnp.zeros((USED, 128), jnp.float32) for _ in range(count)]
        for b in range(blocks):
            term = terms_ref[b]
            for i in range(count):
                totals[i] = totals[i] + weights_ref[first + k + i, b : b + 1, :] * term
        for i in range(count):
            whole = jnp.concatenate([totals[i], jnp.zeros((SLOT - USED, 128), jnp.float32)], axis=0)
            out_ref[(k + i) * SLOT : (k + i + 1) * SLOT, :] = whole.astype(out_ref.dtype)


def rest_kernel(sub_count, terms_ref, weights_ref, near_ref, here_ref):
    write_sums(weights_ref, terms_ref, sub_count, sub_count, near_ref)
    write_sums(weights_ref, terms_ref, 2 * sub_count, sub_count, here_ref)


def project_kernel(kept_ref, got_ref, state_ref, increment_ref, drop_ref):
    total = kept_ref[...] + got_ref[...].astype(jnp.float32)
    row, lane, column, square = lane_patterns(HALF)
    packed = total[:HALF]
    shifted = pltpu.roll(packed, HALF, 1)
    corner = pltpu.roll(jnp.broadcast_to(total[HALF + 1 : HALF + 2], (HALF, 128)), HALF, 1)
    first = lane < 64
    top = packed * jnp.where(square, jnp.where(row < column, 2.0, jnp.where(row == column, 1.0, 0.0)), 2.0)
    bottom = jnp.where(square, 0.0, jnp.where(row > column, 2.0 * shifted, jnp.where(row == column, corner, 0.0)))
    row16, lane16, _, _ = lane_patterns(16)
    weights = jnp.broadcast_to(total[HALF : HALF + 1], (16, 128))
    weights = jnp.where(row16 == lane16 // 64, weights, 0.0)
    mixer = jnp.concatenate(
        [
            jnp.where(first, top, 0.0),
            jnp.where(first, bottom, 0.0),
            jnp.where(first, 0.0, top),
            jnp.where(first, 0.0, bottom),
            weights,
        ],
        axis=0,
    ).astype(jnp.bfloat16)
    width = 512
    for at in range(0, state_ref.shape[1], width):
        state = state_ref[:, at : at + width]
        projected = jnp.dot(mixer, state, preferred_element_type=jnp.float32)
        product = state.astype(jnp.float32) * projected[:128]
        increment_ref[:, at : at + width] = projected[128:130]
        drop_ref[0:1, at : at + width] = jnp.sum(product[:64], axis=0, keepdims=True)
        drop_ref[1:2, at : at + width] = jnp.sum(product[64:], axis=0, keepdims=True)


def local(state_anom, obs_anom, innovations, obs_error, influence, taper_level, obs_count):
    sub_count = lax.axis_size("sub")
    regions = lax.axis_size("region")
    col_blocks, members, cells = state_anom.shape
    blocks = obs_anom.shape[0]
    assert (col_blocks, members, obs_anom.shape[2]) == (2, 64, 128)
    assert regions % 2 == 0 and sub_count & (sub_count - 1) == 0
    vmem = pl.BlockSpec(memory_space=pltpu.VMEM)
    smem = pl.BlockSpec(memory_space=pltpu.SMEM)
    rows = sub_count * SLOT
    terms, weights, far = pl.pallas_call(
        functools.partial(terms_kernel, sub_count, regions),
        out_shape=(
            jax.ShapeDtypeStruct((blocks, USED, 128), jnp.float32),
            jax.ShapeDtypeStruct((3 * sub_count, blocks, 128), jnp.float32),
            jax.ShapeDtypeStruct((rows, 128), jnp.bfloat16),
        ),
        in_specs=[smem] + [vmem] * 5,
        out_specs=(vmem, vmem, vmem),
        scratch_shapes=[pltpu.VMEM((8, 128), jnp.float32)] + [pltpu.VMEM((blocks, 128), jnp.float32)] * 2,
        cost_estimate=pl.CostEstimate(flops=2 * blocks * 80 * 256 * 128, bytes_accessed=blocks * 64 * 128 * 2, transcendentals=0),
    )(obs_count, influence.T, taper_level.T, obs_anom, innovations, obs_error)
    from_far = lax.ppermute(far, "region", [(r, (r + 2 * (r % 2) - 1) % regions) for r in range(regions)])
    near, here = pl.pallas_call(
        functools.partial(rest_kernel, sub_count),
        out_shape=(
            jax.ShapeDtypeStruct((rows, 128), jnp.bfloat16),
            jax.ShapeDtypeStruct((rows, 128), jnp.float32),
        ),
        in_specs=[vmem] * 2,
        out_specs=(vmem, vmem),
        cost_estimate=pl.CostEstimate(flops=4 * blocks * rows * 128, bytes_accessed=blocks * USED * 512, transcendentals=0),
    )(terms, weights)
    from_near = lax.ppermute(near, "region", [(r, r ^ 1) for r in range(regions)])
    total = here + from_near.astype(jnp.float32) + from_far.astype(jnp.float32)
    step = 1
    while step < sub_count:
        half = total.shape[0] // 2
        got = lax.ppermute(total[half:].astype(jnp.bfloat16), "sub", [(s, s ^ step) for s in range(sub_count)])
        kept = total[:half]
        step *= 2
        if step < sub_count:
            total = kept + got.astype(jnp.float32)
    increment, variance_drop = pl.pallas_call(
        project_kernel,
        out_shape=(jax.ShapeDtypeStruct((2, cells), jnp.float32),) * 2,
        in_specs=[vmem] * 3,
        out_specs=(vmem, vmem),
        cost_estimate=pl.CostEstimate(flops=2 * 144 * 128 * cells, bytes_accessed=col_blocks * 64 * cells * 2, transcendentals=0),
    )(kept, got, state_anom.reshape(col_blocks * members, cells))
    return (increment, variance_drop)


def solution(mesh):
    return jax.shard_map(
        local,
        mesh=mesh,
        in_specs=(
            P(AXES, None, None),
            P(AXES, None, None),
            P(AXES, None),
            P(AXES, None),
            P(AXES, None),
            P(AXES, None),
            P("region"),
        ),
        out_specs=(P(AXES, None), P(AXES, None)),
        check_vma=False,
    )
```

time: 88.4 us -> 24.3 us (0.27)
  blocking collectives: 52.8 us -> 0 us
  between operations: 14.8 us -> 1.3 us
  matrix products: 7.34 us -> 0 us
  Pallas kernels: 0 us -> 6.93 us
  starting transfers between devices: 2.73 us -> 8.53 us
  local copies, waits for them, and re-layouts: 4.45 us -> 1.21 us
  waiting for transfers between devices: 2.31 us -> 5.2 us
  other arithmetic: 3.34 us -> 0.92 us
    all_gather x4 -> x0, blocking collectives: 52.8 us -> none  [the longest x1 13.7 us: local(): target_piece = lax.all_gather(influence, 'sub', axis=0, tiled=True)]
    dot_general x4 -> x0, matrix products: 7.34 us -> none  [the longest x1 2.62 us: block_terms(): jnp.einsum('bmo,bno->bmn', scaled, obs_blocks, preferred_element_type=jnp...]
    pallas_call x0 -> x3, Pallas kernels: none -> 6.93 us  [the longest x1 2.54 us: local(): pl.pallas_call(functools.partial(terms_kernel, sub_count, regions), out_s...]
    ppermute x2 -> x4, starting transfers between devices: 2.69 us -> 8.53 us  [the longest x2 4.52 us: local(): lax.ppermute(total[half:].astype(jnp.bfloat16), 'sub', [(s, s ^ step) for...]
    ppermute x2 -> x4, waiting for transfers between devices: 1.61 us -> 5.2 us  [the longest x2 3.43 us: local(): lax.ppermute(total[half:].astype(jnp.bfloat16), 'sub', [(s, s ^ step) for...]
    dot_general x2 -> x0, local copies, waits for them, and re-layouts: 3.16 us -> none  [the longest x1 3.08 us: block_terms(): jnp.einsum('bmo,bno->bmn', scaled, obs_blocks, preferred_element_type=jnp...]
    dot_general x1 -> x0, other arithmetic: 2.06 us -> none  [block_terms(): jnp.einsum('bmo,bmo->bo', obs_blocks, obs_blocks, preferred_element_type=...]
    reduce_sum x2 -> x0, other arithmetic: 1.09 us -> none  [the longest x1 1.07 us: local(): jnp.sum(state_anom.astype(jnp.float32) * projected[:, 1:, :], axis=1)]
  transfers between devices with their start and end apart: 3 -> 4, of which waited for: 1 -> 3; matrix products, arithmetic and copies ran while one was open for 0% -> 2% of each run, Pallas kernels for 0% -> 0%
where the time goes in v1:
time: 24.3 us; the launch traced here: 24.1 us
  starting transfers between devices  8.53 us (35%)
  Pallas kernels  6.93 us (29%)
  waiting for transfers between devices  5.2 us (21%)
  between operations  1.3 us (5%)
  local copies, waits for them, and re-layouts  1.21 us (5%)
  other arithmetic  0.92 us (4%)
    ppermute x2, starting transfers between devices, local(): lax.ppermute(total[half:].astype(jnp.bfloat16), 'sub', [(s, s ^ step) for...  4.52 us
    ppermute x1, starting transfers between devices, local(): lax.ppermute(far, 'region', [(r, (r + 2 * (r % 2) - 1) % regions) for r i...  3.55 us
    ppermute x2, waiting for transfers between devices, local(): lax.ppermute(total[half:].astype(jnp.bfloat16), 'sub', [(s, s ^ step) for...  3.43 us
    pallas_call x1, Pallas kernels, local(): pl.pallas_call(functools.partial(terms_kernel, sub_count, regions), out_s...  2.54 us
    pallas_call x1, Pallas kernels, local(): pl.pallas_call(project_kernel, out_shape=(jax.ShapeDtypeStruct((2, cells)...  2.4 us
    pallas_call x1, Pallas kernels, local(): pl.pallas_call(functools.partial(rest_kernel, sub_count), out_shape=(jax....  1.98 us
    ppermute x1, waiting for transfers between devices, local(): lax.ppermute(far, 'region', [(r, (r + 2 * (r % 2) - 1) % regions) for r i...  1.77 us
    add x1, other arithmetic, local(): total = here + from_near.astype(jnp.float32) + from_far.astype(jnp.float32)  0.91 us
  transfers between devices with their start and end apart: 4, of which 3 were waited for; matrix products, arithmetic and copies ran while one was open for 2% of the time, Pallas kernels for 0%

profile of v1, /device:TPU:0, one launch (start us, length us, event | category | flops | bytes accessed | tf_op | source)
XLA Modules:
  0.0 24.1 jit_solution(4844026234953495114)
XLA Ops:
  1.3 2.5 %shard_map.86 = (f32[24,40,128]{2,1,0:T(8,128)}, f32[12,24,128]{2,1,0:T(8,128)}, bf16[192,128]{1,0:T(8,128)(2,1)}) custom-call(s32[1]{0:T(128)S(6)} %copy.9.count_ref, s32[4,24]{1,0:T(4,128)} %bitcast.4, s32[4,24]{1,0:T(4,128)} %bitcast.5, bf16[24,64,128]{2,1,0:T(8,128)(2,1)} %obs_ref.1, bf16[24,128]{1,0:T(8,128)(2,1)} %innov_ref.1, bf16[24,128]{1,0:T(8,128)(2,1)} %error_ref.1), custom_call_target="tpu_custom_call" | custom-call | flops 125829120 | bytes 393216 | tf_op jit(solution)/shard_map/pallas_call | solution.py:153
  3.8 0.0 copy-start.1
  3.8 2.0 %shard_map.87 = (bf16[192,128]{1,0:T(8,128)(2,1)}, f32[192,128]{1,0:T(8,128)}) custom-call(f32[24,40,128]{2,1,0:T(8,128)} %get-tuple-element.7.terms_ref, f32[12,24,128]{2,1,0:T(8,128)} %get-tuple-element.8.weights_ref), custom_call_target="tpu_custom_call" | custom-call | flops 2359296 | bytes 491520 | tf_op jit(solution)/shard_map/pallas_call | solution.py:166
  5.8 0.5 %collective-permute-start = (bf16[192,128]{1,0:T(8,128)(2,1)}, bf16[192,128]{1,0:T(8,128)(2,1)S(1)}, u32[]{:S(2)}, u32[]{:S(2)}) collective-permute-start(bf16[192,128]{1,0:T(8,128)(2,1)} %get-tuple-element.10), channel_id=1, source_target_pairs={{0,4},{4,0},{8,12},{12,8},{16,20},{20,16},{24,28},{28,24},{1,5},{5... | collective-permute-start | bytes 147464 | tf_op jit(solution)/shard_map/ppermute | solution.py:176
  6.3 0.0 copy-done.1
  6.3 3.5 %collective-permute-start.1 = (bf16[192,128]{1,0:T(8,128)(2,1)S(1)}, bf16[192,128]{1,0:T(8,128)(2,1)S(1)}, u32[]{:S(2)}, u32[]{:S(2)}) collective-permute-start(bf16[192,128]{1,0:T(8,128)(2,1)S(1)} %copy-done.1), channel_id=1, source_target_pairs={{0,28},{4,8},{8,4},{12,16},{16,12},{20,24},{24,20},{28,0},{1,29},{... | collective-permute-start | bytes 147464 | tf_op jit(solution)/shard_map/ppermute | solution.py:165
  9.8 0.0 collective-permute-done
  9.8 1.8 %collective-permute-done.1 = bf16[192,128]{1,0:T(8,128)(2,1)S(1)} collective-permute-done((bf16[192,128]{1,0:T(8,128)(2,1)S(1)}, bf16[192,128]{1,0:T(8,128)(2,1)S(1)}, u32[]{:S(2)}, u32[]{:S(2)}) %collective-permute-start.1) | collective-permute-done | bytes 49184 | tf_op jit(solution)/shard_map/ppermute | solution.py:165
  11.6 0.9 %convert_add_fusion = f32[192,128]{1,0:T(8,128)S(1)} fusion(bf16[192,128]{1,0:T(8,128)(2,1)S(1)} %collective-permute-done.1, f32[192,128]{1,0:T(8,128)} %get-tuple-element.9, bf16[192,128]{1,0:T(8,128)(2,1)S(1)} %collective-permute-done), kind=kLoop, calls=%fused_computation | loop fusion | flops 98304 | bytes 294912 | tf_op jit(solution)/shard_map/add | solution.py:177
  12.5 1.8 %collective-permute-start.2 = (bf16[96,128]{1,0:T(8,128)(2,1)S(1)}, bf16[96,128]{1,0:T(8,128)(2,1)S(1)}, u32[]{:S(2)}, u32[]{:S(2)}) collective-permute-start(bf16[96,128]{1,0:T(8,128)(2,1)S(1)} %slice.25), channel_id=1, source_target_pairs={{0,1},{1,0},{2,3},{3,2},{4,5},{5,4},{6,7},{7,6},{8,9},{9,8},{10,11... | collective-permute-start | bytes 73736 | tf_op jit(solution)/shard_map/ppermute | solution.py:181
  14.3 2.1 %collective-permute-done.2 = bf16[96,128]{1,0:T(8,128)(2,1)S(1)} collective-permute-done((bf16[96,128]{1,0:T(8,128)(2,1)S(1)}, bf16[96,128]{1,0:T(8,128)(2,1)S(1)}, u32[]{:S(2)}, u32[]{:S(2)}) %collective-permute-start.2) | collective-permute-done | bytes 24608 | tf_op jit(solution)/shard_map/ppermute | solution.py:181
  16.4 2.8 %collective-permute-start.3 = (bf16[48,128]{1,0:T(8,128)(2,1)S(1)}, bf16[48,128]{1,0:T(8,128)(2,1)S(1)}, u32[]{:S(2)}, u32[]{:S(2)}) collective-permute-start(bf16[48,128]{1,0:T(8,128)(2,1)S(1)} %slice.26), channel_id=1, source_target_pairs={{0,2},{1,3},{2,0},{3,1},{4,6},{5,7},{6,4},{7,5},{8,10},{9,11},{10,... | collective-permute-start | bytes 36872 | tf_op jit(solution)/shard_map/ppermute | solution.py:181
  19.2 0.6 %slice.20.kept_ref = f32[48,128]{1,0:T(8,128)} slice(f32[96,128]{1,0:T(8,128)S(1)} %slice_add_fusion), slice={[0:48], [0:128]} | slice | bytes 49152 | tf_op jit(solution)/shard_map/slice | solution.py:182
  19.8 1.3 %collective-permute-done.3.got_ref = bf16[48,128]{1,0:T(8,128)(2,1)S(1)} collective-permute-done((bf16[48,128]{1,0:T(8,128)(2,1)S(1)}, bf16[48,128]{1,0:T(8,128)(2,1)S(1)}, u32[]{:S(2)}, u32[]{:S(2)}) %collective-permute-start.3) | collective-permute-done | bytes 12320 | tf_op jit(solution)/shard_map/ppermute | solution.py:181
  21.1 0.0 copy-start
  21.1 0.6 %copy-done = bf16[48,128]{1,0:T(8,128)(2,1)} copy-done((bf16[48,128]{1,0:T(8,128)(2,1)}, bf16[48,128]{1,0:T(8,128)(2,1)S(1)}, u32[]{:S(2)}) %copy-start) | copy-done | bytes 12312
  21.7 2.4 %shard_map.88 = (f32[2,4096]{1,0:T(2,128)}, f32[2,4096]{1,0:T(2,128)}) custom-call(f32[48,128]{1,0:T(8,128)} %slice.20.kept_ref, bf16[48,128]{1,0:T(8,128)(2,1)} %copy-done, bf16[128,4096]{1,0:T(8,128)(2,1)} %bitcast.3), custom_call_target="tpu_custom_call" | custom-call | flops 150994944 | bytes 1048576 | tf_op jit(solution)/shard_map/pallas_call | solution.py:186
  (3 shorter events, 0.0 us)
Async XLA Ops:
  3.8 2.4 %copy-start.1 = (bf16[192,128]{1,0:T(8,128)(2,1)S(1)}, bf16[192,128]{1,0:T(8,128)(2,1)}, u32[]{:S(2)}) copy-start(bf16[192,128]{1,0:T(8,128)(2,1)} %get-tuple-element.11) | copy-start | bytes 147460
  5.8 4.0 %collective-permute-start = (bf16[192,128]{1,0:T(8,128)(2,1)}, bf16[192,128]{1,0:T(8,128)(2,1)S(1)}, u32[]{:S(2)}, u32[]{:S(2)}) collective-permute-start(bf16[192,128]{1,0:T(8,128)(2,1)} %get-tuple-element.10), channel_id=1, source_target_pairs={{0,4},{4,0},{8,12},{12,8},{16,20},{20,16},{24,28},{28,24},{1,5},{5... | collective-permute-start | bytes 147464 | tf_op jit(solution)/shard_map/ppermute | solution.py:176
  6.3 5.3 %collective-permute-start.1 = (bf16[192,128]{1,0:T(8,128)(2,1)S(1)}, bf16[192,128]{1,0:T(8,128)(2,1)S(1)}, u32[]{:S(2)}, u32[]{:S(2)}) collective-permute-start(bf16[192,128]{1,0:T(8,128)(2,1)S(1)} %copy-done.1), channel_id=1, source_target_pairs={{0,28},{4,8},{8,4},{12,16},{16,12},{20,24},{24,20},{28,0},{1,29},{... | collective-permute-start | bytes 147464 | tf_op jit(solution)/shard_map/ppermute | solution.py:165
  12.5 3.9 %collective-permute-start.2 = (bf16[96,128]{1,0:T(8,128)(2,1)S(1)}, bf16[96,128]{1,0:T(8,128)(2,1)S(1)}, u32[]{:S(2)}, u32[]{:S(2)}) collective-permute-start(bf16[96,128]{1,0:T(8,128)(2,1)S(1)} %slice.25), channel_id=1, source_target_pairs={{0,1},{1,0},{2,3},{3,2},{4,5},{5,4},{6,7},{7,6},{8,9},{9,8},{10,11... | collective-permute-start | bytes 73736 | tf_op jit(solution)/shard_map/ppermute | solution.py:181
  16.4 4.7 %collective-permute-start.3 = (bf16[48,128]{1,0:T(8,128)(2,1)S(1)}, bf16[48,128]{1,0:T(8,128)(2,1)S(1)}, u32[]{:S(2)}, u32[]{:S(2)}) collective-permute-start(bf16[48,128]{1,0:T(8,128)(2,1)S(1)} %slice.26), channel_id=1, source_target_pairs={{0,2},{1,3},{2,0},{3,1},{4,6},{5,7},{6,4},{7,5},{8,10},{9,11},{10,... | collective-permute-start | bytes 36872 | tf_op jit(solution)/shard_map/ppermute | solution.py:181
  21.1 0.6 %copy-start = (bf16[48,128]{1,0:T(8,128)(2,1)}, bf16[48,128]{1,0:T(8,128)(2,1)S(1)}, u32[]{:S(2)}) copy-start(bf16[48,128]{1,0:T(8,128)(2,1)S(1)} %collective-permute-done.3.got_ref) | copy-start | bytes 36868

commit v2 on v1

--- a/solution.py
+++ b/solution.py
@@ -11,6 +11,7 @@
 HALF = 32
 SLOT = 48
 USED = 40
+VMEM_LIMIT = 8 * 1024 * 1024
 
 
 def lane_patterns(rows):
@@ -51,9 +52,18 @@
     return here, near, far
 
 
-def terms_kernel(sub_count, regions, count_ref, infl_ref, level_ref, obs_ref, innov_ref, error_ref,
-                 terms_ref, weights_ref, far_ref, rows_ref, error32, innov32):
+def terms_kernel(sub_count, regions, count_ref, infl_hbm, level_hbm, innov_hbm, error_hbm, obs_hbm,
+                 terms_ref, weights_ref, far_ref,
+                 infl_ref, level_ref, innov_ref, error_ref, obs_ref, rows_ref, error32, innov32, small_sems, obs_sem):
     blocks, members, per_block = obs_ref.shape
+    pairs = ((infl_hbm, infl_ref), (level_hbm, level_ref), (innov_hbm, innov_ref), (error_hbm, error_ref))
+    small = [pltpu.make_async_copy(pair[0], pair[1], small_sems.at[i]) for i, pair in enumerate(pairs)]
+    for copy in small:
+        copy.start()
+    large = pltpu.make_async_copy(obs_hbm, obs_ref, obs_sem)
+    large.start()
+    for copy in small:
+        copy.wait()
     here, near, far = neighbours(regions)
     sub_here = lax.axis_index("sub")
     divisor = members - 1.0
@@ -66,6 +76,7 @@
     row8 = lax.broadcasted_iota(jnp.int32, (8, 128), 0)
     place = lax.broadcasted_iota(jnp.int32, (1, 128), 1)
     left = count_ref[0] - sub_here * (blocks * per_block)
+    large.wait()
     for b in range(blocks):
         raw = obs_ref[b]
         values = raw.astype(jnp.float32)
@@ -91,16 +102,17 @@
 
 def write_sums(weights_ref, terms_ref, first, sub_count, out_ref):
     blocks = terms_ref.shape[0]
-    for k in range(0, sub_count, 4):
-        count = min(4, sub_count - k)
-        totals = [jnp.zeros((USED, 128), jnp.float32) for _ in range(count)]
+    stride = out_ref.shape[0] // sub_count
+    rest = [jnp.zeros((stride - USED, 128), jnp.float32)] if stride > USED else []
+    group = min(4, sub_count)
+    for k in range(0, sub_count, group):
+        totals = [jnp.zeros((USED, 128), jnp.float32) for _ in range(group)]
         for b in range(blocks):
             term = terms_ref[b]
-            for i in range(count):
+            for i in range(group):
                 totals[i] = totals[i] + weights_ref[first + k + i, b : b + 1, :] * term
-        for i in range(count):
-            whole = jnp.concatenate([totals[i], jnp.zeros((SLOT - USED, 128), jnp.float32)], axis=0)
-            out_ref[(k + i) * SLOT : (k + i + 1) * SLOT, :] = whole.astype(out_ref.dtype)
+        whole = jnp.concatenate([part for total in totals for part in [total] + rest], axis=0)
+        out_ref[k * stride : (k + group) * stride, :] = whole.astype(out_ref.dtype)
 
 
 def rest_kernel(sub_count, terms_ref, weights_ref, near_ref, here_ref):
@@ -108,8 +120,8 @@
     write_sums(weights_ref, terms_ref, 2 * sub_count, sub_count, here_ref)
 
 
-def project_kernel(kept_ref, got_ref, state_ref, increment_ref, drop_ref):
-    total = kept_ref[...] + got_ref[...].astype(jnp.float32)
+def project_kernel(total_ref, state_ref, increment_ref, drop_ref):
+    total = total_ref[...]
     row, lane, column, square = lane_patterns(HALF)
     packed = total[:HALF]
     shifted = pltpu.roll(packed, HALF, 1)
@@ -140,15 +152,18 @@
         drop_ref[1:2, at : at + width] = jnp.sum(product[64:], axis=0, keepdims=True)
 
 
+def narrow(sums, count):
+    return sums.reshape(count, -1, 128)[:, :USED].astype(jnp.float32)
+
+
 def local(state_anom, obs_anom, innovations, obs_error, influence, taper_level, obs_count):
     sub_count = lax.axis_size("sub")
     regions = lax.axis_size("region")
     col_blocks, members, cells = state_anom.shape
     blocks = obs_anom.shape[0]
     assert (col_blocks, members, obs_anom.shape[2]) == (2, 64, 128)
-    assert regions % 2 == 0 and sub_count & (sub_count - 1) == 0
+    assert regions % 2 == 0 and sub_count in (4, 16, 64)
     vmem = pl.BlockSpec(memory_space=pltpu.VMEM)
-    smem = pl.BlockSpec(memory_space=pltpu.SMEM)
     rows = sub_count * SLOT
     terms, weights, far = pl.pallas_call(
         functools.partial(terms_kernel, sub_count, regions),
@@ -157,39 +172,59 @@
             jax.ShapeDtypeStruct((3 * sub_count, blocks, 128), jnp.float32),
             jax.ShapeDtypeStruct((rows, 128), jnp.bfloat16),
         ),
-        in_specs=[smem] + [vmem] * 5,
+        in_specs=[pl.BlockSpec(memory_space=pltpu.SMEM)] + [pl.BlockSpec(memory_space=pltpu.HBM)] * 5,
         out_specs=(vmem, vmem, vmem),
-        scratch_shapes=[pltpu.VMEM((8, 128), jnp.float32)] + [pltpu.VMEM((blocks, 128), jnp.float32)] * 2,
+        scratch_shapes=[
+            pltpu.VMEM((4, blocks), jnp.int32),
+            pltpu.VMEM((4, blocks), jnp.int32),
+            pltpu.VMEM(innovations.shape, jnp.bfloat16),
+            pltpu.VMEM(obs_error.shape, jnp.bfloat16),
+            pltpu.VMEM(obs_anom.shape, jnp.bfloat16),
+            pltpu.VMEM((8, 128), jnp.float32),
+            pltpu.VMEM((blocks, 128), jnp.float32),
+            pltpu.VMEM((blocks, 128), jnp.float32),
+            pltpu.SemaphoreType.DMA((4,)),
+            pltpu.SemaphoreType.DMA,
+        ],
+        compiler_params=pltpu.CompilerParams(vmem_limit_bytes=VMEM_LIMIT),
         cost_estimate=pl.CostEstimate(flops=2 * blocks * 80 * 256 * 128, bytes_accessed=blocks * 64 * 128 * 2, transcendentals=0),
-    )(obs_count, influence.T, taper_level.T, obs_anom, innovations, obs_error)
+    )(obs_count, *[pltpu.with_memory_space_constraint(x, pltpu.HBM) for x in (influence.T, taper_level.T, innovations, obs_error, obs_anom)])
+    state_anom, far = lax.optimization_barrier((state_anom, far))
     from_far = lax.ppermute(far, "region", [(r, (r + 2 * (r % 2) - 1) % regions) for r in range(regions)])
     near, here = pl.pallas_call(
         functools.partial(rest_kernel, sub_count),
         out_shape=(
-            jax.ShapeDtypeStruct((rows, 128), jnp.bfloat16),
-            jax.ShapeDtypeStruct((rows, 128), jnp.float32),
+            jax.ShapeDtypeStruct((sub_count * USED, 128), jnp.bfloat16),
+            jax.ShapeDtypeStruct((sub_count * USED, 128), jnp.float32),
         ),
         in_specs=[vmem] * 2,
         out_specs=(vmem, vmem),
+        compiler_params=pltpu.CompilerParams(vmem_limit_bytes=VMEM_LIMIT),
         cost_estimate=pl.CostEstimate(flops=4 * blocks * rows * 128, bytes_accessed=blocks * USED * 512, transcendentals=0),
     )(terms, weights)
-    from_near = lax.ppermute(near, "region", [(r, r ^ 1) for r in range(regions)])
-    total = here + from_near.astype(jnp.float32) + from_far.astype(jnp.float32)
+    devices = [(r, s) for r in range(regions) for s in range(sub_count)]
+    place = {device: i for i, device in enumerate(devices)}
+    beside = [(place[r, s], place[r ^ 1, s]) for r, s in devices]
+    from_near = lax.ppermute(near, AXES, beside)
+
+    total = here.reshape(sub_count, USED, 128) + (narrow(from_far, sub_count) + narrow(from_near, sub_count))
     step = 1
     while step < sub_count:
         half = total.shape[0] // 2
-        got = lax.ppermute(total[half:].astype(jnp.bfloat16), "sub", [(s, s ^ step) for s in range(sub_count)])
-        kept = total[:half]
+        sent = jnp.pad(total[half:], ((0, 0), (0, SLOT - USED), (0, 0))).reshape(half * SLOT, 128).astype(jnp.bfloat16)
+        kept = total[:half].reshape(half * USED, 128).astype(jnp.bfloat16)
+        got = lax.ppermute(sent, AXES, [(place[r, s], place[r ^ 1, s ^ step]) for r, s in devices])
+        kept = lax.ppermute(kept, AXES, beside)
+        total = narrow(kept, half) + narrow(got, half)
         step *= 2
-        if step < sub_count:
-            total = kept + got.astype(jnp.float32)
     increment, variance_drop = pl.pallas_call(
         project_kernel,
         out_shape=(jax.ShapeDtypeStruct((2, cells), jnp.float32),) * 2,
-        in_specs=[vmem] * 3,
+        in_specs=[vmem] * 2,
         out_specs=(vmem, vmem),
+        compiler_params=pltpu.CompilerParams(vmem_limit_bytes=VMEM_LIMIT),
         cost_estimate=pl.CostEstimate(flops=2 * 144 * 128 * cells, bytes_accessed=col_blocks * 64 * cells * 2, transcendentals=0),
-    )(kept, got, state_anom.reshape(col_blocks * members, cells))
+    )(total[0], state_anom.reshape(col_blocks * members, cells))
     return (increment, variance_drop)
 
 

time: 24.3 us -> 18.2 us (0.75)
  Pallas kernels: 6.93 us -> 3.24 us
  waiting for transfers between devices: 5.2 us -> 3.27 us
  starting transfers between devices: 8.53 us -> 10 us
  local copies, waits for them, and re-layouts: 1.21 us -> 0.02 us
  other arithmetic: 0.92 us -> 0.03 us
    pallas_call x1, Pallas kernels: 1.98 us -> 0.28 us  [local(): pl.pallas_call(functools.partial(rest_kernel, sub_count), out_shape=(jax....]
    ppermute x3 -> x5, starting transfers between devices: 4.98 us -> 6.61 us  [the longest x2 4.42 us: local(): lax.ppermute(sent, AXES, [(place[r, s], place[r ^ 1, s ^ step]) for r, s...]
    ppermute x1, waiting for transfers between devices: 1.77 us -> 0.21 us  [local(): lax.ppermute(far, 'region', [(r, (r + 2 * (r % 2) - 1) % regions) for r i...]
    pallas_call x1, Pallas kernels: 2.4 us -> 1.14 us  [local(): pl.pallas_call(project_kernel, out_shape=(jax.ShapeDtypeStruct((2, cells)...]
    add x2 -> x0, other arithmetic: 0.92 us -> none  [the longest x1 0.91 us: local(): total = here + from_near.astype(jnp.float32) + from_far.astype(jnp.float32)]
    pallas_call x1, Pallas kernels: 2.54 us -> 1.82 us  [local(): pl.pallas_call(functools.partial(terms_kernel, sub_count, regions), out_s...]
    slice x3 -> x1, local copies, waits for them, and re-layouts: 0.61 us -> 0.01 us  [local(): total[half:]]
    unnamed x4 -> x2, local copies, waits for them, and re-layouts: 0.6 us -> 0.01 us
  transfers between devices with their start and end apart: 4 -> 6, of which waited for: 3 -> 5; matrix products, arithmetic and copies ran while one was open for 2% -> 0% of each run, Pallas kernels for 0% -> 2%
where the time goes in v2:
time: 18.2 us; the launch traced here: 18 us
  starting transfers between devices  10 us (55%)
  waiting for transfers between devices  3.27 us (18%)
  Pallas kernels  3.24 us (18%)
  between operations  1.44 us (8%)
    ppermute x2, starting transfers between devices, local(): lax.ppermute(sent, AXES, [(place[r, s], place[r ^ 1, s ^ step]) for r, s...  4.42 us
    ppermute x1, starting transfers between devices, local(): lax.ppermute(far, 'region', [(r, (r + 2 * (r % 2) - 1) % regions) for r i...  3.4 us
    ppermute x2, starting transfers between devices, local(): kept = lax.ppermute(kept, AXES, beside)  2.12 us
    pallas_call x1, Pallas kernels, local(): pl.pallas_call(functools.partial(terms_kernel, sub_count, regions), out_s...  1.82 us
    ppermute x2, waiting for transfers between devices, local(): kept = lax.ppermute(kept, AXES, beside)  1.68 us
    ppermute x1, waiting for transfers between devices, local(): from_near = lax.ppermute(near, AXES, beside)  1.21 us
    pallas_call x1, Pallas kernels, local(): pl.pallas_call(project_kernel, out_shape=(jax.ShapeDtypeStruct((2, cells)...  1.14 us
  transfers between devices with their start and end apart: 6, of which 5 were waited for; matrix products, arithmetic and copies ran while one was open for 0% of the time, Pallas kernels for 2%

profile of v2, /device:TPU:0, one launch (start us, length us, event | category | flops | bytes accessed | tf_op | source)
XLA Modules:
  0.0 18.0 jit_solution(14005062843231951)
XLA Ops:
  0.6 0.0 copy-start
  1.4 1.8 %shard_map.86 = (f32[24,40,128]{2,1,0:T(8,128)S(1)}, f32[12,24,128]{2,1,0:T(8,128)S(1)}, bf16[192,128]{1,0:T(8,128)(2,1)S(1)}) custom-call(s32[1]{0:T(128)S(6)} %copy.9.count_ref, s32[4,24]{1,0:T(4,128)} %bitcast.31, s32[4,24]{1,0:T(4,128)} %bitcast.32, bf16[24,128]{1,0:T(8,128)(2,1)} %innov_hbm.1, bf16[24,128]{1,0:T(8,128)(2,1)} %error_hbm.1, ...), custom_call_target="tpu_custom_call" | custom-call | flops 125829120 | bytes 393216 | tf_op jit(solution)/shard_map/pallas_call | solution.py:168
  3.2 3.4 %collective-permute-start = (bf16[192,128]{1,0:T(8,128)(2,1)S(1)}, bf16[192,128]{1,0:T(8,128)(2,1)S(1)}, u32[]{:S(2)}, u32[]{:S(2)}) collective-permute-start(bf16[192,128]{1,0:T(8,128)(2,1)S(1)} %get-tuple-element.13), channel_id=1, source_target_pairs={{0,28},{4,8},{8,4},{12,16},{16,12},{20,24},{24,20},{28,0},{1,29},{... | collective-permute-start | bytes 147464 | tf_op jit(solution)/shard_map/ppermute | solution.py:193
  6.6 0.3 %shard_map.87 = (bf16[160,128]{1,0:T(8,128)(2,1)S(1)}, f32[160,128]{1,0:T(8,128)S(1)}) custom-call(f32[24,40,128]{2,1,0:T(8,128)S(1)} %get-tuple-element.9.terms_ref, f32[12,24,128]{2,1,0:T(8,128)S(1)} %get-tuple-element.10.weights_ref), custom_call_target="tpu_custom_call" | custom-call | flops 2359296 | bytes 491520 | tf_op jit(solution)/shard_map/pallas_call | solution.py:194
  6.9 0.1 collective-permute-start.1
  7.0 1.2 %collective-permute-done.1 = bf16[160,128]{1,0:T(8,128)(2,1)S(1)} collective-permute-done((bf16[160,128]{1,0:T(8,128)(2,1)S(1)}, bf16[160,128]{1,0:T(8,128)(2,1)S(1)}, u32[]{:S(2)}, u32[]{:S(2)}) %collective-permute-start.1) | collective-permute-done | bytes 40992 | tf_op jit(solution)/shard_map/ppermute | solution.py:208
  8.2 0.2 %collective-permute-done = bf16[192,128]{1,0:T(8,128)(2,1)S(1)} collective-permute-done((bf16[192,128]{1,0:T(8,128)(2,1)S(1)}, bf16[192,128]{1,0:T(8,128)(2,1)S(1)}, u32[]{:S(2)}, u32[]{:S(2)}) %collective-permute-start) | collective-permute-done | bytes 49184 | tf_op jit(solution)/shard_map/ppermute | solution.py:193
  8.4 1.2 %collective-permute-start.3 = (bf16[96,128]{1,0:T(8,128)(2,1)S(1)}, bf16[96,128]{1,0:T(8,128)(2,1)S(1)}, u32[]{:S(2)}, u32[]{:S(2)}) collective-permute-start(bf16[96,128]{1,0:T(8,128)(2,1)S(1)} %bitcast.26), channel_id=1, source_target_pairs={{0,5},{1,4},{2,7},{3,6},{4,1},{5,0},{6,3},{7,2},{8,13},{9,12},{10,... | collective-permute-start | bytes 73736 | tf_op jit(solution)/shard_map/ppermute | solution.py:216
  9.6 1.7 %collective-permute-start.2 = (bf16[80,128]{1,0:T(8,128)(2,1)S(1)}, bf16[80,128]{1,0:T(8,128)(2,1)S(1)}, u32[]{:S(2)}, u32[]{:S(2)}) collective-permute-start(bf16[80,128]{1,0:T(8,128)(2,1)S(1)} %bitcast.27), channel_id=1, source_target_pairs={{0,4},{1,5},{2,6},{3,7},{4,0},{5,1},{6,2},{7,3},{8,12},{9,13},{10,... | collective-permute-start | bytes 61448 | tf_op jit(solution)/shard_map/ppermute | solution.py:217
  11.4 0.8 %collective-permute-done.2 = bf16[80,128]{1,0:T(8,128)(2,1)S(1)} collective-permute-done((bf16[80,128]{1,0:T(8,128)(2,1)S(1)}, bf16[80,128]{1,0:T(8,128)(2,1)S(1)}, u32[]{:S(2)}, u32[]{:S(2)}) %collective-permute-start.2) | collective-permute-done | bytes 20512 | tf_op jit(solution)/shard_map/ppermute | solution.py:217
  12.2 0.0 collective-permute-done.3
  12.2 3.2 %collective-permute-start.5 = (bf16[48,128]{1,0:T(8,128)(2,1)S(1)}, bf16[48,128]{1,0:T(8,128)(2,1)S(1)}, u32[]{:S(2)}, u32[]{:S(2)}) collective-permute-start(bf16[48,128]{1,0:T(8,128)(2,1)S(1)} %pad_bitcast_fusion), channel_id=1, source_target_pairs={{0,6},{1,7},{2,4},{3,5},{4,2},{5,3},{6,0},{7,1},{8,14},{9,15},{10,... | collective-permute-start | bytes 36872 | tf_op jit(solution)/shard_map/ppermute | solution.py:216
  15.5 0.4 %collective-permute-start.4 = (bf16[40,128]{1,0:T(8,128)(2,1)S(1)}, bf16[40,128]{1,0:T(8,128)(2,1)S(1)}, u32[]{:S(2)}, u32[]{:S(2)}) collective-permute-start(bf16[40,128]{1,0:T(8,128)(2,1)S(1)} %get-tuple-element.18), channel_id=1, source_target_pairs={{0,4},{1,5},{2,6},{3,7},{4,0},{5,1},{6,2},{7,3},{8,12},{9,13},{10,... | collective-permute-start | bytes 30728 | tf_op jit(solution)/shard_map/ppermute | solution.py:217
  15.9 0.8 %collective-permute-done.4 = bf16[40,128]{1,0:T(8,128)(2,1)S(1)} collective-permute-done((bf16[40,128]{1,0:T(8,128)(2,1)S(1)}, bf16[40,128]{1,0:T(8,128)(2,1)S(1)}, u32[]{:S(2)}, u32[]{:S(2)}) %collective-permute-start.4) | collective-permute-done | bytes 10272 | tf_op jit(solution)/shard_map/ppermute | solution.py:217
  16.7 0.2 collective-permute-done.5
  16.9 0.0 copy-done
  16.9 1.1 %shard_map.88 = (f32[2,4096]{1,0:T(2,128)}, f32[2,4096]{1,0:T(2,128)}) custom-call(f32[40,128]{1,0:T(8,128)S(1)} %fusion.3.total_ref, bf16[128,4096]{1,0:T(8,128)(2,1)S(1)} %bitcast.22), custom_call_target="tpu_custom_call" | custom-call | flops 150994944 | bytes 1048576 | tf_op jit(solution)/shard_map/pallas_call | solution.py:220
  (7 shorter events, 0.1 us)
Async XLA Ops:
  0.6 16.2 %copy-start = (bf16[2,64,4096]{2,1,0:T(8,128)(2,1)S(1)}, bf16[2,64,4096]{2,1,0:T(8,128)(2,1)}, u32[]{:S(2)}) copy-start(bf16[2,64,4096]{2,1,0:T(8,128)(2,1)} %param.7) | copy-start | bytes 3145732
  3.2 5.2 %collective-permute-start = (bf16[192,128]{1,0:T(8,128)(2,1)S(1)}, bf16[192,128]{1,0:T(8,128)(2,1)S(1)}, u32[]{:S(2)}, u32[]{:S(2)}) collective-permute-start(bf16[192,128]{1,0:T(8,128)(2,1)S(1)} %get-tuple-element.13), channel_id=1, source_target_pairs={{0,28},{4,8},{8,4},{12,16},{16,12},{20,24},{24,20},{28,0},{1,29},{... | collective-permute-start | bytes 147464 | tf_op jit(solution)/shard_map/ppermute | solution.py:193
  6.9 1.3 %collective-permute-start.1 = (bf16[160,128]{1,0:T(8,128)(2,1)S(1)}, bf16[160,128]{1,0:T(8,128)(2,1)S(1)}, u32[]{:S(2)}, u32[]{:S(2)}) collective-permute-start(bf16[160,128]{1,0:T(8,128)(2,1)S(1)} %get-tuple-element.14), channel_id=1, source_target_pairs={{0,4},{1,5},{2,6},{3,7},{4,0},{5,1},{6,2},{7,3},{8,12},{9,13},{10,... | collective-permute-start | bytes 122888 | tf_op jit(solution)/shard_map/ppermute | solution.py:208
  8.4 3.8 %collective-permute-start.3 = (bf16[96,128]{1,0:T(8,128)(2,1)S(1)}, bf16[96,128]{1,0:T(8,128)(2,1)S(1)}, u32[]{:S(2)}, u32[]{:S(2)}) collective-permute-start(bf16[96,128]{1,0:T(8,128)(2,1)S(1)} %bitcast.26), channel_id=1, source_target_pairs={{0,5},{1,4},{2,7},{3,6},{4,1},{5,0},{6,3},{7,2},{8,13},{9,12},{10,... | collective-permute-start | bytes 73736 | tf_op jit(solution)/shard_map/ppermute | solution.py:216
  9.6 2.6 %collective-permute-start.2 = (bf16[80,128]{1,0:T(8,128)(2,1)S(1)}, bf16[80,128]{1,0:T(8,128)(2,1)S(1)}, u32[]{:S(2)}, u32[]{:S(2)}) collective-permute-start(bf16[80,128]{1,0:T(8,128)(2,1)S(1)} %bitcast.27), channel_id=1, source_target_pairs={{0,4},{1,5},{2,6},{3,7},{4,0},{5,1},{6,2},{7,3},{8,12},{9,13},{10,... | collective-permute-start | bytes 61448 | tf_op jit(solution)/shard_map/ppermute | solution.py:217
  12.2 4.6 %collective-permute-start.5 = (bf16[48,128]{1,0:T(8,128)(2,1)S(1)}, bf16[48,128]{1,0:T(8,128)(2,1)S(1)}, u32[]{:S(2)}, u32[]{:S(2)}) collective-permute-start(bf16[48,128]{1,0:T(8,128)(2,1)S(1)} %pad_bitcast_fusion), channel_id=1, source_target_pairs={{0,6},{1,7},{2,4},{3,5},{4,2},{5,3},{6,0},{7,1},{8,14},{9,15},{10,... | collective-permute-start | bytes 36872 | tf_op jit(solution)/shard_map/ppermute | solution.py:216
  15.5 1.2 %collective-permute-start.4 = (bf16[40,128]{1,0:T(8,128)(2,1)S(1)}, bf16[40,128]{1,0:T(8,128)(2,1)S(1)}, u32[]{:S(2)}, u32[]{:S(2)}) collective-permute-start(bf16[40,128]{1,0:T(8,128)(2,1)S(1)} %get-tuple-element.18), channel_id=1, source_target_pairs={{0,4},{1,5},{2,6},{3,7},{4,0},{5,1},{6,2},{7,3},{8,12},{9,13},{10,... | collective-permute-start | bytes 30728 | tf_op jit(solution)/shard_map/ppermute | solution.py:217

commit v3 on v1

--- a/solution.py
+++ b/solution.py
@@ -9,8 +9,9 @@
 
 AXES = ("region", "sub")
 HALF = 32
-SLOT = 48
 USED = 40
+HEAD_COST = pl.CostEstimate(flops=10**10, bytes_accessed=10**8, transcendentals=0)
+VMEM_LIMIT = 8 * 1024 * 1024
 
 
 def lane_patterns(rows):
@@ -51,7 +52,11 @@
     return here, near, far
 
 
-def terms_kernel(sub_count, regions, count_ref, infl_ref, level_ref, obs_ref, innov_ref, error_ref,
+def place_kernel(out_ref):
+    out_ref[...] = lax.broadcasted_iota(jnp.int32, (1, 128), 1)
+
+
+def terms_kernel(sub_count, regions, count_ref, place_ref, infl_ref, level_ref, innov_ref, error_ref, obs_ref,
                  terms_ref, weights_ref, far_ref, rows_ref, error32, innov32):
     blocks, members, per_block = obs_ref.shape
     here, near, far = neighbours(regions)
@@ -64,7 +69,7 @@
     upper = (row <= column) | ~square
     diagonal = (row == column) & square
     row8 = lax.broadcasted_iota(jnp.int32, (8, 128), 0)
-    place = lax.broadcasted_iota(jnp.int32, (1, 128), 1)
+    place = place_ref[...]
     left = count_ref[0] - sub_here * (blocks * per_block)
     for b in range(blocks):
         raw = obs_ref[b]
@@ -84,23 +89,30 @@
         lower = product[HALF : 2 * HALF, 128:]
         terms_ref[b, 0:HALF, :] = jnp.where(upper, product[:HALF, :128], lower)
         corner = jnp.sum(jnp.where(diagonal, lower, 0.0), axis=0, keepdims=True)
-        extra = jnp.where(row8 == 0, divisor * product[2 * HALF : 2 * HALF + 8, :128], jnp.where(row8 == 1, corner, 0.0))
+        extra = jnp.where(row8 % 2 == 0, divisor * product[2 * HALF : 2 * HALF + 8, :128], corner)
         terms_ref[b, HALF:USED, :] = extra
     write_sums(weights_ref, terms_ref, 0, sub_count, far_ref)
 
 
 def write_sums(weights_ref, terms_ref, first, sub_count, out_ref):
     blocks = terms_ref.shape[0]
+    pair = lax.broadcasted_iota(jnp.int32, (8, 128), 0) // 2
+    matrices, extras = [], []
     for k in range(0, sub_count, 4):
-        count = min(4, sub_count - k)
-        totals = [jnp.zeros((USED, 128), jnp.float32) for _ in range(count)]
+        totals = [jnp.zeros((USED, 128), jnp.float32) for _ in range(4)]
         for b in range(blocks):
             term = terms_ref[b]
-            for i in range(count):
+            for i in range(4):
                 totals[i] = totals[i] + weights_ref[first + k + i, b : b + 1, :] * term
-        for i in range(count):
-            whole = jnp.concatenate([totals[i], jnp.zeros((SLOT - USED, 128), jnp.float32)], axis=0)
-            out_ref[(k + i) * SLOT : (k + i + 1) * SLOT, :] = whole.astype(out_ref.dtype)
+        matrices += [total[:HALF] for total in totals]
+        extra = totals[3][HALF:]
+        for i in range(3):
+            extra = jnp.where(pair == i, totals[i][HALF:], extra)
+        extras.append(extra)
+    rest = out_ref.shape[0] - sub_count * (HALF + 2)
+    if rest:
+        extras.append(jnp.zeros((rest, 128), jnp.float32))
+    out_ref[...] = jnp.concatenate(matrices + extras, axis=0).astype(out_ref.dtype)
 
 
 def rest_kernel(sub_count, terms_ref, weights_ref, near_ref, here_ref):
@@ -108,17 +120,40 @@
     write_sums(weights_ref, terms_ref, 2 * sub_count, sub_count, here_ref)
 
 
+def added(count, refs):
+    total = sum(ref[...].astype(jnp.float32)[: sum_rows(count, 8)] for ref in refs)
+    return total[: count * HALF], total[count * HALF :]
+
+
+def sum_rows(count, multiple):
+    return count * HALF + -(-2 * count // multiple) * multiple
+
+
+def fold_kernel(count, *refs):
+    *sums, sent_ref, kept_ref = refs
+    matrix, extra = added(count, sums)
+    half = count // 2
+    if half % 4:
+        high = pltpu.roll(extra, 8 - 2 * half, 0)
+        low = extra
+    else:
+        low, high = extra[: 2 * half], extra[2 * half :]
+    fill = sent_ref.shape[0] - sum_rows(half, 8)
+    pad = [jnp.zeros((fill, 128), jnp.float32)] if fill else []
+    sent_ref[...] = jnp.concatenate([matrix[half * HALF :], high] + pad, axis=0).astype(sent_ref.dtype)
+    kept_ref[...] = jnp.concatenate([matrix[: half * HALF], low], axis=0).astype(kept_ref.dtype)
+
+
 def project_kernel(kept_ref, got_ref, state_ref, increment_ref, drop_ref):
-    total = kept_ref[...] + got_ref[...].astype(jnp.float32)
+    matrix, extra = added(1, (kept_ref, got_ref))
     row, lane, column, square = lane_patterns(HALF)
-    packed = total[:HALF]
-    shifted = pltpu.roll(packed, HALF, 1)
-    corner = pltpu.roll(jnp.broadcast_to(total[HALF + 1 : HALF + 2], (HALF, 128)), HALF, 1)
+    shifted = pltpu.roll(matrix, HALF, 1)
+    corner = pltpu.roll(jnp.broadcast_to(extra[1:2], (HALF, 128)), HALF, 1)
     first = lane < 64
-    top = packed * jnp.where(square, jnp.where(row < column, 2.0, jnp.where(row == column, 1.0, 0.0)), 2.0)
+    top = matrix * jnp.where(square, jnp.where(row < column, 2.0, jnp.where(row == column, 1.0, 0.0)), 2.0)
     bottom = jnp.where(square, 0.0, jnp.where(row > column, 2.0 * shifted, jnp.where(row == column, corner, 0.0)))
     row16, lane16, _, _ = lane_patterns(16)
-    weights = jnp.broadcast_to(total[HALF : HALF + 1], (16, 128))
+    weights = jnp.broadcast_to(extra[0:1], (16, 128))
     weights = jnp.where(row16 == lane16 // 64, weights, 0.0)
     mixer = jnp.concatenate(
         [
@@ -146,10 +181,17 @@
     col_blocks, members, cells = state_anom.shape
     blocks = obs_anom.shape[0]
     assert (col_blocks, members, obs_anom.shape[2]) == (2, 64, 128)
-    assert regions % 2 == 0 and sub_count & (sub_count - 1) == 0
+    assert regions % 2 == 0 and sub_count in (4, 16, 64)
     vmem = pl.BlockSpec(memory_space=pltpu.VMEM)
-    smem = pl.BlockSpec(memory_space=pltpu.SMEM)
-    rows = sub_count * SLOT
+    rows = sum_rows(sub_count, 16)
+    place = pl.pallas_call(
+        place_kernel,
+        out_shape=jax.ShapeDtypeStruct((1, 128), jnp.int32),
+        out_specs=vmem,
+        compiler_params=pltpu.CompilerParams(vmem_limit_bytes=VMEM_LIMIT),
+        cost_estimate=HEAD_COST,
+    )()
+    obs_count, place = lax.optimization_barrier((obs_count, place))
     terms, weights, far = pl.pallas_call(
         functools.partial(terms_kernel, sub_count, regions),
         out_shape=(
@@ -157,39 +199,58 @@
             jax.ShapeDtypeStruct((3 * sub_count, blocks, 128), jnp.float32),
             jax.ShapeDtypeStruct((rows, 128), jnp.bfloat16),
         ),
-        in_specs=[smem] + [vmem] * 5,
+        in_specs=[pl.BlockSpec(memory_space=pltpu.SMEM)] + [vmem] * 6,
         out_specs=(vmem, vmem, vmem),
-        scratch_shapes=[pltpu.VMEM((8, 128), jnp.float32)] + [pltpu.VMEM((blocks, 128), jnp.float32)] * 2,
+        scratch_shapes=[
+            pltpu.VMEM((8, 128), jnp.float32),
+            pltpu.VMEM((blocks, 128), jnp.float32),
+            pltpu.VMEM((blocks, 128), jnp.float32),
+        ],
+        compiler_params=pltpu.CompilerParams(vmem_limit_bytes=VMEM_LIMIT),
         cost_estimate=pl.CostEstimate(flops=2 * blocks * 80 * 256 * 128, bytes_accessed=blocks * 64 * 128 * 2, transcendentals=0),
-    )(obs_count, influence.T, taper_level.T, obs_anom, innovations, obs_error)
+    )(obs_count, place, influence.T, taper_level.T, innovations, obs_error, obs_anom)
+    state_anom, far = lax.optimization_barrier((state_anom, far))
     from_far = lax.ppermute(far, "region", [(r, (r + 2 * (r % 2) - 1) % regions) for r in range(regions)])
     near, here = pl.pallas_call(
         functools.partial(rest_kernel, sub_count),
         out_shape=(
-            jax.ShapeDtypeStruct((rows, 128), jnp.bfloat16),
-            jax.ShapeDtypeStruct((rows, 128), jnp.float32),
+            jax.ShapeDtypeStruct((sum_rows(sub_count, 8), 128), jnp.bfloat16),
+            jax.ShapeDtypeStruct((sum_rows(sub_count, 8), 128), jnp.float32),
         ),
         in_specs=[vmem] * 2,
         out_specs=(vmem, vmem),
+        compiler_params=pltpu.CompilerParams(vmem_limit_bytes=VMEM_LIMIT),
         cost_estimate=pl.CostEstimate(flops=4 * blocks * rows * 128, bytes_accessed=blocks * USED * 512, transcendentals=0),
     )(terms, weights)
-    from_near = lax.ppermute(near, "region", [(r, r ^ 1) for r in range(regions)])
-    total = here + from_near.astype(jnp.float32) + from_far.astype(jnp.float32)
-    step = 1
+    devices = [(r, s) for r in range(regions) for s in range(sub_count)]
+    index = {device: i for i, device in enumerate(devices)}
+    beside = [(index[r, s], index[r ^ 1, s]) for r, s in devices]
+    from_near = lax.ppermute(near, AXES, beside)
+
+    sums = (here, from_far, from_near)
+    step, count = 1, sub_count
     while step < sub_count:
-        half = total.shape[0] // 2
-        got = lax.ppermute(total[half:].astype(jnp.bfloat16), "sub", [(s, s ^ step) for s in range(sub_count)])
-        kept = total[:half]
-        step *= 2
-        if step < sub_count:
-            total = kept + got.astype(jnp.float32)
+        half = count // 2
+        sent, kept = pl.pallas_call(
+            functools.partial(fold_kernel, count),
+            out_shape=tuple(jax.ShapeDtypeStruct((sum_rows(half, m), 128), jnp.bfloat16) for m in (16, 8)),
+            in_specs=[vmem] * len(sums),
+            out_specs=(vmem, vmem),
+            compiler_params=pltpu.CompilerParams(vmem_limit_bytes=VMEM_LIMIT),
+            cost_estimate=pl.CostEstimate(flops=count * 64 * 128, bytes_accessed=count * 64 * 1024, transcendentals=0),
+        )(*sums)
+        got = lax.ppermute(sent, AXES, [(index[r, s], index[r ^ 1, s ^ step]) for r, s in devices])
+        kept = lax.ppermute(kept, AXES, beside)
+        sums = (kept, got)
+        step, count = 2 * step, half
     increment, variance_drop = pl.pallas_call(
         project_kernel,
         out_shape=(jax.ShapeDtypeStruct((2, cells), jnp.float32),) * 2,
         in_specs=[vmem] * 3,
         out_specs=(vmem, vmem),
+        compiler_params=pltpu.CompilerParams(vmem_limit_bytes=VMEM_LIMIT),
         cost_estimate=pl.CostEstimate(flops=2 * 144 * 128 * cells, bytes_accessed=col_blocks * 64 * cells * 2, transcendentals=0),
-    )(kept, got, state_anom.reshape(col_blocks * members, cells))
+    )(*sums, state_anom.reshape(col_blocks * members, cells))
     return (increment, variance_drop)
 
 

time: 24.3 us -> 16.9 us (0.70)
  Pallas kernels: 6.93 us -> 2.22 us
  waiting for transfers between devices: 5.2 us -> 3.09 us
  starting transfers between devices: 8.53 us -> 9.79 us
  local copies, waits for them, and re-layouts: 1.21 us -> 0.21 us
  other arithmetic: 0.92 us -> 0 us
    pallas_call x1, Pallas kernels: 2.54 us -> 0.72 us  [local(): pl.pallas_call(functools.partial(terms_kernel, sub_count, regions), out_s...]
    ppermute x1, waiting for transfers between devices: 1.77 us -> 0.04 us  [local(): lax.ppermute(far, 'region', [(r, (r + 2 * (r % 2) - 1) % regions) for r i...]
    pallas_call x1, Pallas kernels: 1.98 us -> 0.33 us  [local(): pl.pallas_call(functools.partial(rest_kernel, sub_count), out_shape=(jax....]
    ppermute x3 -> x5, starting transfers between devices: 4.98 us -> 6.39 us  [the longest x2 4.51 us: local(): lax.ppermute(sent, AXES, [(index[r, s], index[r ^ 1, s ^ step]) for r, s...]
    pallas_call x1, Pallas kernels: 2.4 us -> 1.14 us  [local(): pl.pallas_call(project_kernel, out_shape=(jax.ShapeDtypeStruct((2, cells)...]
    add x2 -> x0, other arithmetic: 0.92 us -> none  [the longest x1 0.91 us: local(): total = here + from_near.astype(jnp.float32) + from_far.astype(jnp.float32)]
    slice x3 -> x0, local copies, waits for them, and re-layouts: 0.61 us -> none  [the longest x1 0.6 us: local(): kept = total[:half]]
    unnamed x4 -> x12, local copies, waits for them, and re-layouts: 0.6 us -> 0.21 us
  transfers between devices with their start and end apart: 4 -> 6, of which waited for: 3 -> 4; matrix products, arithmetic and copies ran while one was open for 2% -> 0% of each run, Pallas kernels for 0% -> 2%
where the time goes in v3:
time: 16.9 us; the launch traced here: 16.8 us
  starting transfers between devices  9.79 us (58%)
  waiting for transfers between devices  3.09 us (18%)
  Pallas kernels  2.22 us (13%)
  between operations  1.48 us (9%)
  local copies, waits for them, and re-layouts  0.21 us (1%)
    ppermute x2, starting transfers between devices, local(): lax.ppermute(sent, AXES, [(index[r, s], index[r ^ 1, s ^ step]) for r, s...  4.51 us
    ppermute x1, starting transfers between devices, local(): lax.ppermute(far, 'region', [(r, (r + 2 * (r % 2) - 1) % regions) for r i...  3.4 us
    ppermute x2, starting transfers between devices, local(): kept = lax.ppermute(kept, AXES, beside)  1.81 us
    ppermute x2, waiting for transfers between devices, local(): kept = lax.ppermute(kept, AXES, beside)  1.67 us
    ppermute x1, waiting for transfers between devices, local(): from_near = lax.ppermute(near, AXES, beside)  1.2 us
    pallas_call x1, Pallas kernels, local(): pl.pallas_call(project_kernel, out_shape=(jax.ShapeDtypeStruct((2, cells)...  1.14 us
    pallas_call x1, Pallas kernels, local(): pl.pallas_call(functools.partial(terms_kernel, sub_count, regions), out_s...  0.72 us
  transfers between devices with their start and end apart: 6, of which 4 were waited for; matrix products, arithmetic and copies ran while one was open for 0% of the time, Pallas kernels for 2%

profile of v3, /device:TPU:0, one launch (start us, length us, event | category | flops | bytes accessed | tf_op | source)
XLA Modules:
  0.0 16.8 jit_solution(1240635845063616591)
XLA Ops:
  0.6 0.0 copy-start.3
  0.6 0.0 copy-start.2
  0.7 0.0 copy-start.1
  0.7 0.0 copy-start.4
  0.7 0.0 copy-start.5
  0.7 0.0 copy-start
  1.5 0.0 copy-done.3
  1.5 0.0 copy-done.2
  1.5 0.2 %copy-done.1 = bf16[24,64,128]{2,1,0:T(8,128)(2,1)S(1)} copy-done((bf16[24,64,128]{2,1,0:T(8,128)(2,1)S(1)}, bf16[24,64,128]{2,1,0:T(8,128)(2,1)}, u32[]{:S(2)}) %copy-start.1) | copy-done | bytes 393240
  1.7 0.0 copy-done.4
  1.7 0.0 copy-done.5
  1.7 0.7 %shard_map.87 = (f32[24,40,128]{2,1,0:T(8,128)S(1)}, f32[12,24,128]{2,1,0:T(8,128)S(1)}, bf16[144,128]{1,0:T(8,128)(2,1)S(1)}) custom-call(s32[1]{0:T(128)S(6)} %copy.9.count_ref, s32[1,128]{1,0:T(1,128)S(1)} %shard_map.86.place_ref, s32[4,24]{1,0:T(4,128)S(1)} %bitcast.4, s32[4,24]{1,0:T(4,128)S(1)} %bitcast.5, bf16[24,128]{1,0:T(8,128)(2,1)S(1)} %copy-done.2, ...), custom_call_target="tpu_custom_call" | custom-call | flops 125829120 | bytes 393216 | tf_op jit(solution)/shard_map/pallas_call | solution.py:195
  2.4 3.4 %collective-permute-start = (bf16[144,128]{1,0:T(8,128)(2,1)S(1)}, bf16[144,128]{1,0:T(8,128)(2,1)S(1)}, u32[]{:S(2)}, u32[]{:S(2)}) collective-permute-start(bf16[144,128]{1,0:T(8,128)(2,1)S(1)} %get-tuple-element.21), channel_id=1, source_target_pairs={{0,28},{4,8},{8,4},{12,16},{16,12},{20,24},{24,20},{28,0},{1,29},{... | collective-permute-start | bytes 110600 | tf_op jit(solution)/shard_map/ppermute | solution.py:213
  5.8 0.3 %shard_map.88 = (bf16[136,128]{1,0:T(8,128)(2,1)S(1)}, f32[136,128]{1,0:T(8,128)S(1)}) custom-call(f32[24,40,128]{2,1,0:T(8,128)S(1)} %get-tuple-element.17.terms_ref, f32[12,24,128]{2,1,0:T(8,128)S(1)} %get-tuple-element.18.weights_ref), custom_call_target="tpu_custom_call" | custom-call | flops 1769472 | bytes 491520 | tf_op jit(solution)/shard_map/pallas_call | solution.py:214
  6.1 0.1 collective-permute-start.1
  6.2 1.2 %collective-permute-done.1.refs_2_ = bf16[136,128]{1,0:T(8,128)(2,1)S(1)} collective-permute-done((bf16[136,128]{1,0:T(8,128)(2,1)S(1)}, bf16[136,128]{1,0:T(8,128)(2,1)S(1)}, u32[]{:S(2)}, u32[]{:S(2)}) %collective-permute-start.1) | collective-permute-done | bytes 34848 | tf_op jit(solution)/shard_map/ppermute | solution.py:228
  7.4 0.0 collective-permute-done.refs_1_
  7.5 1.4 %collective-permute-start.3 = (bf16[80,128]{1,0:T(8,128)(2,1)S(1)}, bf16[80,128]{1,0:T(8,128)(2,1)S(1)}, u32[]{:S(2)}, u32[]{:S(2)}) collective-permute-start(bf16[80,128]{1,0:T(8,128)(2,1)S(1)} %get-tuple-element.24), channel_id=1, source_target_pairs={{0,5},{1,4},{2,7},{3,6},{4,1},{5,0},{6,3},{7,2},{8,13},{9,12},{10,... | collective-permute-start | bytes 61448 | tf_op jit(solution)/shard_map/ppermute | solution.py:242
  8.8 1.4 %collective-permute-start.2 = (bf16[72,128]{1,0:T(8,128)(2,1)S(1)}, bf16[72,128]{1,0:T(8,128)(2,1)S(1)}, u32[]{:S(2)}, u32[]{:S(2)}) collective-permute-start(bf16[72,128]{1,0:T(8,128)(2,1)S(1)} %get-tuple-element.23), channel_id=1, source_target_pairs={{0,4},{1,5},{2,6},{3,7},{4,0},{5,1},{6,2},{7,3},{8,12},{9,13},{10,... | collective-permute-start | bytes 55304 | tf_op jit(solution)/shard_map/ppermute | solution.py:243
  10.3 0.8 %collective-permute-done.2.refs_0_ = bf16[72,128]{1,0:T(8,128)(2,1)S(1)} collective-permute-done((bf16[72,128]{1,0:T(8,128)(2,1)S(1)}, bf16[72,128]{1,0:T(8,128)(2,1)S(1)}, u32[]{:S(2)}, u32[]{:S(2)}) %collective-permute-start.2) | collective-permute-done | bytes 18464 | tf_op jit(solution)/shard_map/ppermute | solution.py:243
  11.1 0.0 collective-permute-done.3.refs_1_
  11.1 3.1 %collective-permute-start.5 = (bf16[48,128]{1,0:T(8,128)(2,1)S(1)}, bf16[48,128]{1,0:T(8,128)(2,1)S(1)}, u32[]{:S(2)}, u32[]{:S(2)}) collective-permute-start(bf16[48,128]{1,0:T(8,128)(2,1)S(1)} %get-tuple-element.26), channel_id=1, source_target_pairs={{0,6},{1,7},{2,4},{3,5},{4,2},{5,3},{6,0},{7,1},{8,14},{9,15},{10,... | collective-permute-start | bytes 36872 | tf_op jit(solution)/shard_map/ppermute | solution.py:242
  14.2 0.4 %collective-permute-start.4 = (bf16[40,128]{1,0:T(8,128)(2,1)S(1)}, bf16[40,128]{1,0:T(8,128)(2,1)S(1)}, u32[]{:S(2)}, u32[]{:S(2)}) collective-permute-start(bf16[40,128]{1,0:T(8,128)(2,1)S(1)} %get-tuple-element.25), channel_id=1, source_target_pairs={{0,4},{1,5},{2,6},{3,7},{4,0},{5,1},{6,2},{7,3},{8,12},{9,13},{10,... | collective-permute-start | bytes 30728 | tf_op jit(solution)/shard_map/ppermute | solution.py:243
  14.6 0.8 %collective-permute-done.4.kept_ref = bf16[40,128]{1,0:T(8,128)(2,1)S(1)} collective-permute-done((bf16[40,128]{1,0:T(8,128)(2,1)S(1)}, bf16[40,128]{1,0:T(8,128)(2,1)S(1)}, u32[]{:S(2)}, u32[]{:S(2)}) %collective-permute-start.4) | collective-permute-done | bytes 10272 | tf_op jit(solution)/shard_map/ppermute | solution.py:243
  15.5 0.2 %collective-permute-done.5.got_ref = bf16[48,128]{1,0:T(8,128)(2,1)S(1)} collective-permute-done((bf16[48,128]{1,0:T(8,128)(2,1)S(1)}, bf16[48,128]{1,0:T(8,128)(2,1)S(1)}, u32[]{:S(2)}, u32[]{:S(2)}) %collective-permute-start.5) | collective-permute-done | bytes 12320 | tf_op jit(solution)/shard_map/ppermute | solution.py:242
  15.6 0.0 copy-done
  15.6 1.1 %shard_map.91 = (f32[2,4096]{1,0:T(2,128)}, f32[2,4096]{1,0:T(2,128)}) custom-call(bf16[40,128]{1,0:T(8,128)(2,1)S(1)} %collective-permute-done.4.kept_ref, bf16[48,128]{1,0:T(8,128)(2,1)S(1)} %collective-permute-done.5.got_ref, bf16[128,4096]{1,0:T(8,128)(2,1)S(1)} %bitcast.3), custom_call_target="tpu_custom_call" | custom-call | flops 150994944 | bytes 1048576 | tf_op jit(solution)/shard_map/pallas_call | solution.py:246
  (3 shorter events, 0.0 us)
Async XLA Ops:
  0.6 0.8 %copy-start.3 = (bf16[24,128]{1,0:T(8,128)(2,1)S(1)}, bf16[24,128]{1,0:T(8,128)(2,1)}, u32[]{:S(2)}) copy-start(bf16[24,128]{1,0:T(8,128)(2,1)} %error_ref.1) | copy-start | bytes 18436
  0.6 0.8 %copy-start.2 = (bf16[24,128]{1,0:T(8,128)(2,1)S(1)}, bf16[24,128]{1,0:T(8,128)(2,1)}, u32[]{:S(2)}) copy-start(bf16[24,128]{1,0:T(8,128)(2,1)} %innov_ref.1) | copy-start | bytes 18436
  0.7 1.0 %copy-start.1 = (bf16[24,64,128]{2,1,0:T(8,128)(2,1)S(1)}, bf16[24,64,128]{2,1,0:T(8,128)(2,1)}, u32[]{:S(2)}) copy-start(bf16[24,64,128]{2,1,0:T(8,128)(2,1)} %obs_ref.1) | copy-start | bytes 1179652
  0.7 1.0 %copy-start.4 = (s32[24,4]{0,1:T(4,128)S(1)}, s32[24,4]{0,1:T(4,128)}, u32[]{:S(2)}) copy-start(s32[24,4]{0,1:T(4,128)} %param.11) | copy-start | bytes 1156
  0.7 1.0 %copy-start.5 = (s32[24,4]{0,1:T(4,128)S(1)}, s32[24,4]{0,1:T(4,128)}, u32[]{:S(2)}) copy-start(s32[24,4]{0,1:T(4,128)} %param.12) | copy-start | bytes 1156
  0.7 15.0 %copy-start = (bf16[2,64,4096]{2,1,0:T(8,128)(2,1)S(1)}, bf16[2,64,4096]{2,1,0:T(8,128)(2,1)}, u32[]{:S(2)}) copy-start(bf16[2,64,4096]{2,1,0:T(8,128)(2,1)} %param.7) | copy-start | bytes 3145732
  2.4 5.0 %collective-permute-start = (bf16[144,128]{1,0:T(8,128)(2,1)S(1)}, bf16[144,128]{1,0:T(8,128)(2,1)S(1)}, u32[]{:S(2)}, u32[]{:S(2)}) collective-permute-start(bf16[144,128]{1,0:T(8,128)(2,1)S(1)} %get-tuple-element.21), channel_id=1, source_target_pairs={{0,28},{4,8},{8,4},{12,16},{16,12},{20,24},{24,20},{28,0},{1,29},{... | collective-permute-start | bytes 110600 | tf_op jit(solution)/shard_map/ppermute | solution.py:213
  6.1 1.3 %collective-permute-start.1 = (bf16[136,128]{1,0:T(8,128)(2,1)S(1)}, bf16[136,128]{1,0:T(8,128)(2,1)S(1)}, u32[]{:S(2)}, u32[]{:S(2)}) collective-permute-start(bf16[136,128]{1,0:T(8,128)(2,1)S(1)} %get-tuple-element.22), channel_id=1, source_target_pairs={{0,4},{1,5},{2,6},{3,7},{4,0},{5,1},{6,2},{7,3},{8,12},{9,13},{10,... | collective-permute-start | bytes 104456 | tf_op jit(solution)/shard_map/ppermute | solution.py:228
  7.5 3.6 %collective-permute-start.3 = (bf16[80,128]{1,0:T(8,128)(2,1)S(1)}, bf16[80,128]{1,0:T(8,128)(2,1)S(1)}, u32[]{:S(2)}, u32[]{:S(2)}) collective-permute-start(bf16[80,128]{1,0:T(8,128)(2,1)S(1)} %get-tuple-element.24), channel_id=1, source_target_pairs={{0,5},{1,4},{2,7},{3,6},{4,1},{5,0},{6,3},{7,2},{8,13},{9,12},{10,... | collective-permute-start | bytes 61448 | tf_op jit(solution)/shard_map/ppermute | solution.py:242
  8.8 2.3 %collective-permute-start.2 = (bf16[72,128]{1,0:T(8,128)(2,1)S(1)}, bf16[72,128]{1,0:T(8,128)(2,1)S(1)}, u32[]{:S(2)}, u32[]{:S(2)}) collective-permute-start(bf16[72,128]{1,0:T(8,128)(2,1)S(1)} %get-tuple-element.23), channel_id=1, source_target_pairs={{0,4},{1,5},{2,6},{3,7},{4,0},{5,1},{6,2},{7,3},{8,12},{9,13},{10,... | collective-permute-start | bytes 55304 | tf_op jit(solution)/shard_map/ppermute | solution.py:243
  11.1 4.5 %collective-permute-start.5 = (bf16[48,128]{1,0:T(8,128)(2,1)S(1)}, bf16[48,128]{1,0:T(8,128)(2,1)S(1)}, u32[]{:S(2)}, u32[]{:S(2)}) collective-permute-start(bf16[48,128]{1,0:T(8,128)(2,1)S(1)} %get-tuple-element.26), channel_id=1, source_target_pairs={{0,6},{1,7},{2,4},{3,5},{4,2},{5,3},{6,0},{7,1},{8,14},{9,15},{10,... | collective-permute-start | bytes 36872 | tf_op jit(solution)/shard_map/ppermute | solution.py:242
  14.2 1.2 %collective-permute-start.4 = (bf16[40,128]{1,0:T(8,128)(2,1)S(1)}, bf16[40,128]{1,0:T(8,128)(2,1)S(1)}, u32[]{:S(2)}, u32[]{:S(2)}) collective-permute-start(bf16[40,128]{1,0:T(8,128)(2,1)S(1)} %get-tuple-element.25), channel_id=1, source_target_pairs={{0,4},{1,5},{2,6},{3,7},{4,0},{5,1},{6,2},{7,3},{8,12},{9,13},{10,... | collective-permute-start | bytes 30728 | tf_op jit(solution)/shard_map/ppermute | solution.py:243

commit v4 on v3

v4 whole, which is shorter than its diff:
```python
import functools

import jax
import jax.numpy as jnp
from jax import lax
from jax.experimental import pallas as pl
from jax.experimental.pallas import tpu as pltpu
from jax.sharding import PartitionSpec as P

AXES = ("region", "sub")
HALF = 32
USED = 40
HEAD_COST = pl.CostEstimate(flops=10**10, bytes_accessed=10**8, transcendentals=0)
VMEM_LIMIT = 8 * 1024 * 1024


def lane_patterns(rows):
    row = lax.broadcasted_iota(jnp.int32, (rows, 128), 0)
    lane = lax.broadcasted_iota(jnp.int32, (rows, 128), 1)
    return row, lane, lane % HALF, (lane // HALF) % 2 == 0


def pack_weights(infl_ref, level_ref, rows_ref, weights_ref, group_regions, sub_here, sub_count):
    blocks = infl_ref.shape[1]
    rows_ref[...] = jnp.zeros_like(rows_ref)
    rows_ref[0:4, 0:blocks] = infl_ref[...].astype(jnp.float32)
    rows_ref[4:8, 0:blocks] = 1.0 - 0.25 * level_ref[...].astype(jnp.float32)
    columns = rows_ref[...].T
    targets = [jnp.broadcast_to(columns[0:blocks, n : n + 1], (blocks, 128)) for n in range(4)]
    tapers = [jnp.broadcast_to(columns[0:blocks, 4 + n : 5 + n], (blocks, 128)) for n in range(4)]
    local = lax.broadcasted_iota(jnp.int32, (blocks, 128), 1) // 64
    for g, region in enumerate(group_regions):
        for k, slot in enumerate(slot_order(sub_count)):
            first = (region * sub_count + (sub_here ^ slot)) * 2
            wanted = (first + local).astype(jnp.float32)
            weight = jnp.zeros((blocks, 128), jnp.float32)
            for n in range(4):
                weight = weight + jnp.where(targets[n] == wanted, tapers[n], 0.0)
            weights_ref[g * sub_count + k] = weight


def slot_order(sub_count):
    bits = sub_count.bit_length() - 1
    return sorted(range(sub_count), key=lambda i: [(i >> b) & 1 for b in range(bits)])


def neighbours(regions):
    here = lax.axis_index("region")
    odd = here % 2
    far = (here + 2 * odd - 1 + regions) % regions
    near = here + 1 - 2 * odd
    return here, near, far


def place_kernel(out_ref):
    out_ref[...] = lax.broadcasted_iota(jnp.int32, (1, 128), 1)


def terms_kernel(sub_count, regions, count_ref, place_ref, infl_ref, level_ref, innov_ref, error_ref, obs_ref,
                 terms_ref, weights_ref, far_ref, far_later_ref, rows_ref, error32, innov32):
    blocks, members, per_block = obs_ref.shape
    here, near, far = neighbours(regions)
    sub_here = lax.axis_index("sub")
    divisor = members - 1.0
    error32[...] = error_ref[...].astype(jnp.float32)
    innov32[...] = innov_ref[...].astype(jnp.float32)
    pack_weights(infl_ref, level_ref, rows_ref, weights_ref, (far, near, here), sub_here, sub_count)
    row, lane, column, even = lane_patterns(HALF)
    from_top = jnp.where(even, row - column, column - row) <= 0
    diagonal = (row == column) & ~even
    row8 = lax.broadcasted_iota(jnp.int32, (8, 128), 0)
    place = place_ref[...]
    left = count_ref[0] - sub_here * (blocks * per_block)
    for first in range(0, blocks, 2):
        raws, twice, innovs = [], [], []
        for b in (first, first + 1):
            raw = obs_ref[b]
            values = raw.astype(jnp.float32)
            spread = jnp.sum(values * values, axis=0, keepdims=True) / divisor
            usable = jnp.where(place + b * per_block < left, 1.0 / (divisor * divisor), 0.0)
            factor = usable / (spread + error32[b : b + 1, :])
            scaled = (values * factor).astype(jnp.bfloat16)
            raws.append(raw)
            twice += [scaled, scaled]
            innovs.append(jnp.broadcast_to(innov32[b : b + 1, :], (8, 128)))
        rows = raws + [jnp.concatenate(innovs, axis=0).astype(jnp.bfloat16)]
        products = lax.dot_general(
            jnp.concatenate(rows, axis=0),
            jnp.concatenate(twice, axis=0),
            (((1,), (1,)), ((), ())),
            preferred_element_type=jnp.float32,
        )
        for i in range(2):
            product = products[:, i * 128 : (i + 1) * 128]
            top = product[2 * i * HALF : (2 * i + 1) * HALF]
            bottom = product[(2 * i + 1) * HALF : (2 * i + 2) * HALF]
            weight = divisor * product[4 * HALF + 8 * i : 4 * HALF + 8 * (i + 1)]
            corner = jnp.sum(jnp.where(diagonal, bottom, 0.0), axis=0, keepdims=True)
            terms_ref[first + i, 0:HALF, :] = jnp.where(from_top, top, bottom)
            terms_ref[first + i, HALF:USED, :] = jnp.where(row8 % 2 == 0, weight, corner)
    write_sums(weights_ref, terms_ref, sub_count // 2, sub_count // 2, far_ref)
    write_sums(weights_ref, terms_ref, 0, sub_count // 2, far_later_ref)


def write_sums(weights_ref, terms_ref, first, count, out_ref):
    blocks = terms_ref.shape[0]
    pair = lax.broadcasted_iota(jnp.int32, (8, 128), 0) // 2
    matrices, extras = [], []
    group = min(4, count)
    for k in range(0, count, group):
        totals = [jnp.zeros((USED, 128), jnp.float32) for _ in range(group)]
        for b in range(blocks):
            term = terms_ref[b]
            for i in range(group):
                totals[i] = totals[i] + weights_ref[first + k + i, b : b + 1, :] * term
        matrices += [total[:HALF] for total in totals]
        extra = totals[group - 1][HALF:]
        for i in range(group - 1):
            extra = jnp.where(pair == i, totals[i][HALF:], extra)
        extras.append(extra)
    out_ref[...] = jnp.concatenate(matrices + extras, axis=0)[: out_ref.shape[0]].astype(out_ref.dtype)


def near_kernel(sub_count, terms_ref, weights_ref, near_ref):
    write_sums(weights_ref, terms_ref, sub_count + sub_count // 2, sub_count // 2, near_ref)


def rest_kernel(sub_count, terms_ref, weights_ref, here_ref, beside_ref, later_ref):
    half = sub_count // 2
    write_sums(weights_ref, terms_ref, 2 * sub_count + half, half, here_ref)
    write_sums(weights_ref, terms_ref, 2 * sub_count, half, beside_ref)
    write_sums(weights_ref, terms_ref, sub_count, half, later_ref)


def join_kernel(count, *refs):
    *sums, sent_ref, scratch = refs
    sent_ref[...] = jnp.concatenate(added(count, sums, scratch), axis=0).astype(sent_ref.dtype)


def added(count, refs, scratch):
    total = sum(padded(ref, count, scratch) for ref in refs)
    return total[: count * HALF], total[count * HALF :]


def sum_rows(count, multiple):
    return count * HALF + -(-2 * count // multiple) * multiple


def padded(ref, count, scratch):
    rows = sum_rows(count, 8)
    sums = ref[...].astype(jnp.float32)
    if sums.shape[0] >= rows:
        return sums[:rows]
    scratch[: sums.shape[0], :] = sums
    return scratch[:rows, :]


def fold_kernel(count, *refs):
    *sums, sent_ref, kept_ref, scratch = refs
    matrix, extra = added(count, sums, scratch)
    half = count // 2
    if half % 4:
        high = pltpu.roll(extra, 8 - 2 * half, 0)
        low = extra
    else:
        low, high = extra[: 2 * half], extra[2 * half :]
    going = matrix[half * HALF :]
    sent_ref[...] = jnp.concatenate([going, high], axis=0).astype(sent_ref.dtype)
    kept = jnp.concatenate([matrix[: half * HALF], low], axis=0)
    kept_ref[...] = kept[: kept_ref.shape[0]].astype(kept_ref.dtype)


def project_kernel(kept_ref, got_ref, state_ref, increment_ref, drop_ref, scratch):
    matrix, extra = added(1, (kept_ref, got_ref), scratch)
    row, lane, column, even = lane_patterns(HALF)
    first = lane < 64
    place = jnp.where(even, row - column, column - row)
    top = matrix * jnp.where(place < 0, 2.0, jnp.where(place == 0, jnp.where(even, 1.0, 2.0), 0.0))
    bottom = jnp.where(place > 0, 2.0 * matrix, jnp.where((place == 0) & ~even, extra[1:2], 0.0))
    row16, lane16, _, _ = lane_patterns(16)
    weights = jnp.broadcast_to(extra[0:1], (16, 128))
    weights = jnp.where(row16 == lane16 // 64, weights, 0.0)
    mixer = jnp.concatenate(
        [
            jnp.where(first, top, 0.0),
            jnp.where(first, bottom, 0.0),
            jnp.where(first, 0.0, top),
            jnp.where(first, 0.0, bottom),
            weights,
        ],
        axis=0,
    ).astype(jnp.bfloat16)
    width = 512
    for at in range(0, state_ref.shape[1], width):
        state = state_ref[:, at : at + width]
        projected = jnp.dot(mixer, state, preferred_element_type=jnp.float32)
        product = state.astype(jnp.float32) * projected[:128]
        increment_ref[:, at : at + width] = projected[128:130]
        drop_ref[0:1, at : at + width] = jnp.sum(product[:64], axis=0, keepdims=True)
        drop_ref[1:2, at : at + width] = jnp.sum(product[64:], axis=0, keepdims=True)


def local(state_anom, obs_anom, innovations, obs_error, influence, taper_level, obs_count):
    sub_count = lax.axis_size("sub")
    regions = lax.axis_size("region")
    col_blocks, members, cells = state_anom.shape
    blocks = obs_anom.shape[0]
    assert (col_blocks, members, obs_anom.shape[2]) == (2, 64, 128)
    assert regions % 2 == 0 and sub_count in (4, 16, 64)
    vmem = pl.BlockSpec(memory_space=pltpu.VMEM)
    half = sub_count // 2
    wide, narrow = sum_rows(half, 8), sum_rows(half, 2)
    params = pltpu.CompilerParams(vmem_limit_bytes=VMEM_LIMIT)

    def sums(rows, dtype=jnp.bfloat16):
        return jax.ShapeDtypeStruct((rows, 128), dtype)

    place = pl.pallas_call(
        place_kernel,
        out_shape=jax.ShapeDtypeStruct((1, 128), jnp.int32),
        out_specs=vmem,
        compiler_params=pltpu.CompilerParams(vmem_limit_bytes=VMEM_LIMIT),
        cost_estimate=HEAD_COST,
    )()
    obs_count, place = lax.optimization_barrier((obs_count, place))
    terms, weights, far, far_later = pl.pallas_call(
        functools.partial(terms_kernel, sub_count, regions),
        out_shape=(
            jax.ShapeDtypeStruct((blocks, USED, 128), jnp.float32),
            jax.ShapeDtypeStruct((3 * sub_count, blocks, 128), jnp.float32),
            sums(wide),
            sums(wide),
        ),
        in_specs=[pl.BlockSpec(memory_space=pltpu.SMEM)] + [vmem] * 6,
        out_specs=(vmem,) * 4,
        scratch_shapes=[
            pltpu.VMEM((8, 128), jnp.float32),
            pltpu.VMEM((blocks, 128), jnp.float32),
            pltpu.VMEM((blocks, 128), jnp.float32),
        ],
        compiler_params=pltpu.CompilerParams(vmem_limit_bytes=VMEM_LIMIT),
        cost_estimate=pl.CostEstimate(flops=2 * blocks * 80 * 256 * 128, bytes_accessed=blocks * 64 * 128 * 2, transcendentals=0),
    )(obs_count, place, influence.T, taper_level.T, innovations, obs_error, obs_anom)
    state_anom, far = lax.optimization_barrier((state_anom, far))
    devices = [(r, s) for r in range(regions) for s in range(sub_count)]
    index = {device: i for i, device in enumerate(devices)}

    def moved(x, region_to, step=0):
        return lax.ppermute(x, AXES, [(index[r, s], index[region_to(r), s ^ step]) for r, s in devices])

    def sibling(r):
        return r ^ 1

    def across(r):
        return (r + 2 * (r % 2) - 1) % regions

    from_far = moved(far, across)
    from_far_later = moved(far_later, lambda r: sibling(across(r)))
    near = pl.pallas_call(
        functools.partial(near_kernel, sub_count),
        out_shape=sums(narrow),
        in_specs=[vmem] * 2,
        out_specs=vmem,
        compiler_params=params,
        cost_estimate=pl.CostEstimate(flops=blocks * wide * 256, bytes_accessed=blocks * USED * 512, transcendentals=0),
    )(terms, weights)
    from_near = moved(near, sibling)
    here, beside, later = pl.pallas_call(
        functools.partial(rest_kernel, sub_count),
        out_shape=(sums(wide, jnp.float32), sums(narrow), sums(wide, jnp.float32)),
        in_specs=[vmem] * 2,
        out_specs=(vmem,) * 3,
        compiler_params=params,
        cost_estimate=pl.CostEstimate(flops=3 * blocks * wide * 256, bytes_accessed=blocks * USED * 512, transcendentals=0),
    )(terms, weights)
    sent = pl.pallas_call(
        functools.partial(join_kernel, half),
        out_shape=sums(wide),
        in_specs=[vmem] * 3,
        out_specs=vmem,
        scratch_shapes=[pltpu.VMEM((wide, 128), jnp.float32)],
        compiler_params=params,
        cost_estimate=pl.CostEstimate(flops=wide * 256, bytes_accessed=wide * 1024, transcendentals=0),
    )(from_near, here, from_far)
    got = moved(sent, sibling, 1)
    parts = (moved(beside, sibling), got, later, from_far_later)
    step, count = 2, half
    while step < sub_count:
        sent, kept = pl.pallas_call(
            functools.partial(fold_kernel, count),
            out_shape=(sums(sum_rows(count // 2, 8)), sums(sum_rows(count // 2, 2))),
            in_specs=[vmem] * len(parts),
            out_specs=(vmem, vmem),
            scratch_shapes=[pltpu.VMEM((sum_rows(count, 8), 128), jnp.float32)],
            compiler_params=params,
            cost_estimate=pl.CostEstimate(flops=count * 64 * 128, bytes_accessed=count * 64 * 1024, transcendentals=0),
        )(*parts)
        got = moved(sent, sibling, step)
        parts = (moved(kept, sibling), got)
        step, count = 2 * step, count // 2
    increment, variance_drop = pl.pallas_call(
        project_kernel,
        out_shape=(jax.ShapeDtypeStruct((2, cells), jnp.float32),) * 2,
        in_specs=[vmem] * 3,
        out_specs=(vmem, vmem),
        scratch_shapes=[pltpu.VMEM((sum_rows(1, 8), 128), jnp.float32)],
        compiler_params=pltpu.CompilerParams(vmem_limit_bytes=VMEM_LIMIT),
        cost_estimate=pl.CostEstimate(flops=2 * 144 * 128 * cells, bytes_accessed=col_blocks * 64 * cells * 2, transcendentals=0),
    )(*parts, state_anom.reshape(col_blocks * members, cells))
    return (increment, variance_drop)


def solution(mesh):
    return jax.shard_map(
        local,
        mesh=mesh,
        in_specs=(
            P(AXES, None, None),
            P(AXES, None, None),
            P(AXES, None),
            P(AXES, None),
            P(AXES, None),
            P(AXES, None),
            P("region"),
        ),
        out_specs=(P(AXES, None), P(AXES, None)),
        check_vma=False,
    )
```

time: 16.9 us -> 16.2 us (0.959)
  waiting for transfers between devices: 3.09 us -> 2.24 us
  starting transfers between devices: 9.79 us -> 10.1 us
  Pallas kernels: 2.22 us -> 1.97 us
    ppermute x6 -> x7, waiting for transfers between devices: 3.09 us -> 2.24 us  [moved(): lax.ppermute(x, AXES, [(index[r, s], index[region_to(r), s ^ step]) for r...]
    ppermute x6 -> x7, starting transfers between devices: 9.79 us -> 10.1 us  [moved(): lax.ppermute(x, AXES, [(index[r, s], index[region_to(r), s ^ step]) for r...]
    pallas_call x1, Pallas kernels: 0.72 us -> 0.5 us  [local(): pl.pallas_call(functools.partial(terms_kernel, sub_count, regions), out_s...]
    pallas_call x3 -> x4, Pallas kernels: 0.35 us -> 0.38 us  [the longest x1 0.26 us: local(): pl.pallas_call(functools.partial(rest_kernel, sub_count), out_shape=(sums...]
  transfers between devices with their start and end apart: 6 -> 7, of which waited for: 4 -> 5; matrix products, arithmetic and copies ran while one was open for 0% -> 0% of each run, Pallas kernels for 2% -> 2%
where the time goes in v4:
time: 16.2 us; the launch traced here: 16 us
  starting transfers between devices  10.1 us (62%)
  waiting for transfers between devices  2.24 us (14%)
  Pallas kernels  1.97 us (12%)
  between operations  1.48 us (9%)
  local copies, waits for them, and re-layouts  0.21 us (1%)
    ppermute x7, starting transfers between devices, moved(): lax.ppermute(x, AXES, [(index[r, s], index[region_to(r), s ^ step]) for r...  10.1 us
    ppermute x7, waiting for transfers between devices, moved(): lax.ppermute(x, AXES, [(index[r, s], index[region_to(r), s ^ step]) for r...  2.24 us
    pallas_call x1, Pallas kernels, local(): pl.pallas_call(project_kernel, out_shape=(jax.ShapeDtypeStruct((2, cells)...  1.09 us
    pallas_call x1, Pallas kernels, local(): pl.pallas_call(functools.partial(terms_kernel, sub_count, regions), out_s...  0.5 us
  transfers between devices with their start and end apart: 7, of which 5 were waited for; matrix products, arithmetic and copies ran while one was open for 0% of the time, Pallas kernels for 2%

profile of v4, /device:TPU:0, one launch (start us, length us, event | category | flops | bytes accessed | tf_op | source)
XLA Modules:
  0.0 16.0 jit_solution(4250042264446034606)
XLA Ops:
  0.6 0.0 copy-start.3
  0.6 0.0 copy-start.2
  0.7 0.0 copy-start.1
  0.7 0.0 copy-start.4
  0.7 0.0 copy-start.5
  0.7 0.0 copy-start
  1.5 0.0 copy-done.3
  1.5 0.0 copy-done.2
  1.5 0.2 %copy-done.1 = bf16[24,64,128]{2,1,0:T(8,128)(2,1)S(1)} copy-done((bf16[24,64,128]{2,1,0:T(8,128)(2,1)S(1)}, bf16[24,64,128]{2,1,0:T(8,128)(2,1)}, u32[]{:S(2)}) %copy-start.1) | copy-done | bytes 393240
  1.7 0.0 copy-done.4
  1.7 0.0 copy-done.5
  1.7 0.5 %shard_map.87 = (f32[24,40,128]{2,1,0:T(8,128)S(1)}, f32[12,24,128]{2,1,0:T(8,128)S(1)}, bf16[72,128]{1,0:T(8,128)(2,1)S(1)}, bf16[72,128]{1,0:T(8,128)(2,1)S(1)}) custom-call(s32[1]{0:T(128)S(6)} %copy.9.count_ref, s32[1,128]{1,0:T(1,128)S(1)} %shard_map.86.place_ref, s32[4,24]{1,0:T(4,128)S(1)} %bitcast.4, s32[4,24]{1,0:T(4,128)S(1)} %bitcast.5, ...), custom_call_target="tpu_custom_call" | custom-call | flops 125829120 | bytes 393216 | tf_op jit(solution)/shard_map/pallas_call | solution.py:226
  2.2 3.4 %collective-permute-start.2 = (bf16[72,128]{1,0:T(8,128)(2,1)S(1)}, bf16[72,128]{1,0:T(8,128)(2,1)S(1)}, u32[]{:S(2)}, u32[]{:S(2)}) collective-permute-start(bf16[72,128]{1,0:T(8,128)(2,1)S(1)} %get-tuple-element.22), channel_id=1, source_target_pairs={{0,28},{1,29},{2,30},{3,31},{4,8},{5,9},{6,10},{7,11},{8,4},{9,5},... | collective-permute-start | bytes 55304 | tf_op jit(solution)/shard_map/ppermute | solution.py:249
  5.6 0.1 shard_map.89
  5.7 0.1 collective-permute-start.1
  5.8 0.6 %collective-permute-start.4 = (bf16[72,128]{1,0:T(8,128)(2,1)S(1)}, bf16[72,128]{1,0:T(8,128)(2,1)S(1)}, u32[]{:S(2)}, u32[]{:S(2)}) collective-permute-start(bf16[72,128]{1,0:T(8,128)(2,1)S(1)} %get-tuple-element.24), channel_id=1, source_target_pairs={{0,24},{1,25},{2,26},{3,27},{4,12},{5,13},{6,14},{7,15},{8,0},{9,1... | collective-permute-start | bytes 55304 | tf_op jit(solution)/shard_map/ppermute | solution.py:249
  6.4 0.3 %shard_map.88 = (f32[72,128]{1,0:T(8,128)S(1)}, bf16[68,128]{1,0:T(8,128)(2,1)S(1)}, f32[72,128]{1,0:T(8,128)S(1)}) custom-call(f32[24,40,128]{2,1,0:T(8,128)S(1)} %get-tuple-element.17.terms_ref, f32[12,24,128]{2,1,0:T(8,128)S(1)} %get-tuple-element.18.weights_ref), custom_call_target="tpu_custom_call" | custom-call | flops 1327104 | bytes 491520 | tf_op jit(solution)/shard_map/pallas_call | solution.py:268
  6.6 0.3 %collective-permute-done.1.refs_0_ = bf16[68,128]{1,0:T(8,128)(2,1)S(1)} collective-permute-done((bf16[68,128]{1,0:T(8,128)(2,1)S(1)}, bf16[68,128]{1,0:T(8,128)(2,1)S(1)}, u32[]{:S(2)}, u32[]{:S(2)}) %collective-permute-start.1) | collective-permute-done | bytes 17440 | tf_op jit(solution)/shard_map/ppermute | solution.py:249
  6.9 0.1 collective-permute-done.2.refs_2_
  7.1 1.3 %collective-permute-start.3 = (bf16[72,128]{1,0:T(8,128)(2,1)S(1)}, bf16[72,128]{1,0:T(8,128)(2,1)S(1)}, u32[]{:S(2)}, u32[]{:S(2)}) collective-permute-start(bf16[72,128]{1,0:T(8,128)(2,1)S(1)} %shard_map.90), channel_id=1, source_target_pairs={{0,5},{1,4},{2,7},{3,6},{4,1},{5,0},{6,3},{7,2},{8,13},{9,12},{10,... | collective-permute-start | bytes 55304 | tf_op jit(solution)/shard_map/ppermute | solution.py:249
  8.4 1.3 %collective-permute-start = (bf16[68,128]{1,0:T(8,128)(2,1)S(1)}, bf16[68,128]{1,0:T(8,128)(2,1)S(1)}, u32[]{:S(2)}, u32[]{:S(2)}) collective-permute-start(bf16[68,128]{1,0:T(8,128)(2,1)S(1)} %get-tuple-element.19), channel_id=1, source_target_pairs={{0,4},{1,5},{2,6},{3,7},{4,0},{5,1},{6,2},{7,3},{8,12},{9,13},{10,... | collective-permute-start | bytes 52232 | tf_op jit(solution)/shard_map/ppermute | solution.py:249
  9.6 0.8 %collective-permute-done.refs_0_ = bf16[68,128]{1,0:T(8,128)(2,1)S(1)} collective-permute-done((bf16[68,128]{1,0:T(8,128)(2,1)S(1)}, bf16[68,128]{1,0:T(8,128)(2,1)S(1)}, u32[]{:S(2)}, u32[]{:S(2)}) %collective-permute-start) | collective-permute-done | bytes 17440 | tf_op jit(solution)/shard_map/ppermute | solution.py:249
  10.5 0.0 collective-permute-done.4.refs_3_
  10.5 0.0 collective-permute-done.3.refs_1_
  10.5 3.1 %collective-permute-start.6 = (bf16[40,128]{1,0:T(8,128)(2,1)S(1)}, bf16[40,128]{1,0:T(8,128)(2,1)S(1)}, u32[]{:S(2)}, u32[]{:S(2)}) collective-permute-start(bf16[40,128]{1,0:T(8,128)(2,1)S(1)} %get-tuple-element.26), channel_id=1, source_target_pairs={{0,6},{1,7},{2,4},{3,5},{4,2},{5,3},{6,0},{7,1},{8,14},{9,15},{10,... | collective-permute-start | bytes 30728 | tf_op jit(solution)/shard_map/ppermute | solution.py:249
  13.6 0.4 %collective-permute-start.5 = (bf16[34,128]{1,0:T(8,128)(2,1)S(1)}, bf16[34,128]{1,0:T(8,128)(2,1)S(1)}, u32[]{:S(2)}, u32[]{:S(2)}) collective-permute-start(bf16[34,128]{1,0:T(8,128)(2,1)S(1)} %get-tuple-element.25), channel_id=1, source_target_pairs={{0,4},{1,5},{2,6},{3,7},{4,0},{5,1},{6,2},{7,3},{8,12},{9,13},{10,... | collective-permute-start | bytes 26120 | tf_op jit(solution)/shard_map/ppermute | solution.py:249
  14.0 0.8 %collective-permute-done.5.kept_ref = bf16[34,128]{1,0:T(8,128)(2,1)S(1)} collective-permute-done((bf16[34,128]{1,0:T(8,128)(2,1)S(1)}, bf16[34,128]{1,0:T(8,128)(2,1)S(1)}, u32[]{:S(2)}, u32[]{:S(2)}) %collective-permute-start.5) | collective-permute-done | bytes 8736 | tf_op jit(solution)/shard_map/ppermute | solution.py:249
  14.8 0.2 collective-permute-done.6.got_ref
  14.9 0.0 copy-done
  15.0 1.1 %shard_map.92 = (f32[2,4096]{1,0:T(2,128)}, f32[2,4096]{1,0:T(2,128)}) custom-call(bf16[34,128]{1,0:T(8,128)(2,1)S(1)} %collective-permute-done.5.kept_ref, bf16[40,128]{1,0:T(8,128)(2,1)S(1)} %collective-permute-done.6.got_ref, bf16[128,4096]{1,0:T(8,128)(2,1)S(1)} %bitcast.3), custom_call_target="tpu_custom_call" | custom-call | flops 150994944 | bytes 1048576 | tf_op jit(solution)/shard_map/pallas_call | solution.py:301
  (3 shorter events, 0.0 us)
Async XLA Ops:
  0.6 0.8 %copy-start.3 = (bf16[24,128]{1,0:T(8,128)(2,1)S(1)}, bf16[24,128]{1,0:T(8,128)(2,1)}, u32[]{:S(2)}) copy-start(bf16[24,128]{1,0:T(8,128)(2,1)} %error_ref.1) | copy-start | bytes 18436
  0.6 0.8 %copy-start.2 = (bf16[24,128]{1,0:T(8,128)(2,1)S(1)}, bf16[24,128]{1,0:T(8,128)(2,1)}, u32[]{:S(2)}) copy-start(bf16[24,128]{1,0:T(8,128)(2,1)} %innov_ref.1) | copy-start | bytes 18436
  0.7 1.0 %copy-start.1 = (bf16[24,64,128]{2,1,0:T(8,128)(2,1)S(1)}, bf16[24,64,128]{2,1,0:T(8,128)(2,1)}, u32[]{:S(2)}) copy-start(bf16[24,64,128]{2,1,0:T(8,128)(2,1)} %obs_ref.1) | copy-start | bytes 1179652
  0.7 1.0 %copy-start.4 = (s32[24,4]{0,1:T(4,128)S(1)}, s32[24,4]{0,1:T(4,128)}, u32[]{:S(2)}) copy-start(s32[24,4]{0,1:T(4,128)} %param.11) | copy-start | bytes 1156
  0.7 1.0 %copy-start.5 = (s32[24,4]{0,1:T(4,128)S(1)}, s32[24,4]{0,1:T(4,128)}, u32[]{:S(2)}) copy-start(s32[24,4]{0,1:T(4,128)} %param.12) | copy-start | bytes 1156
  0.7 14.3 %copy-start = (bf16[2,64,4096]{2,1,0:T(8,128)(2,1)S(1)}, bf16[2,64,4096]{2,1,0:T(8,128)(2,1)}, u32[]{:S(2)}) copy-start(bf16[2,64,4096]{2,1,0:T(8,128)(2,1)} %param.7) | copy-start | bytes 3145732
  2.2 4.9 %collective-permute-start.2 = (bf16[72,128]{1,0:T(8,128)(2,1)S(1)}, bf16[72,128]{1,0:T(8,128)(2,1)S(1)}, u32[]{:S(2)}, u32[]{:S(2)}) collective-permute-start(bf16[72,128]{1,0:T(8,128)(2,1)S(1)} %get-tuple-element.22), channel_id=1, source_target_pairs={{0,28},{1,29},{2,30},{3,31},{4,8},{5,9},{6,10},{7,11},{8,4},{9,5},... | collective-permute-start | bytes 55304 | tf_op jit(solution)/shard_map/ppermute | solution.py:249
  5.7 1.3 %collective-permute-start.1 = (bf16[68,128]{1,0:T(8,128)(2,1)S(1)}, bf16[68,128]{1,0:T(8,128)(2,1)S(1)}, u32[]{:S(2)}, u32[]{:S(2)}) collective-permute-start(bf16[68,128]{1,0:T(8,128)(2,1)S(1)} %shard_map.89), channel_id=1, source_target_pairs={{0,4},{1,5},{2,6},{3,7},{4,0},{5,1},{6,2},{7,3},{8,12},{9,13},{10,... | collective-permute-start | bytes 52232 | tf_op jit(solution)/shard_map/ppermute | solution.py:249
  5.8 4.7 %collective-permute-start.4 = (bf16[72,128]{1,0:T(8,128)(2,1)S(1)}, bf16[72,128]{1,0:T(8,128)(2,1)S(1)}, u32[]{:S(2)}, u32[]{:S(2)}) collective-permute-start(bf16[72,128]{1,0:T(8,128)(2,1)S(1)} %get-tuple-element.24), channel_id=1, source_target_pairs={{0,24},{1,25},{2,26},{3,27},{4,12},{5,13},{6,14},{7,15},{8,0},{9,1... | collective-permute-start | bytes 55304 | tf_op jit(solution)/shard_map/ppermute | solution.py:249
  7.1 3.4 %collective-permute-start.3 = (bf16[72,128]{1,0:T(8,128)(2,1)S(1)}, bf16[72,128]{1,0:T(8,128)(2,1)S(1)}, u32[]{:S(2)}, u32[]{:S(2)}) collective-permute-start(bf16[72,128]{1,0:T(8,128)(2,1)S(1)} %shard_map.90), channel_id=1, source_target_pairs={{0,5},{1,4},{2,7},{3,6},{4,1},{5,0},{6,3},{7,2},{8,13},{9,12},{10,... | collective-permute-start | bytes 55304 | tf_op jit(solution)/shard_map/ppermute | solution.py:249
  8.4 2.1 %collective-permute-start = (bf16[68,128]{1,0:T(8,128)(2,1)S(1)}, bf16[68,128]{1,0:T(8,128)(2,1)S(1)}, u32[]{:S(2)}, u32[]{:S(2)}) collective-permute-start(bf16[68,128]{1,0:T(8,128)(2,1)S(1)} %get-tuple-element.19), channel_id=1, source_target_pairs={{0,4},{1,5},{2,6},{3,7},{4,0},{5,1},{6,2},{7,3},{8,12},{9,13},{10,... | collective-permute-start | bytes 52232 | tf_op jit(solution)/shard_map/ppermute | solution.py:249
  10.5 4.5 %collective-permute-start.6 = (bf16[40,128]{1,0:T(8,128)(2,1)S(1)}, bf16[40,128]{1,0:T(8,128)(2,1)S(1)}, u32[]{:S(2)}, u32[]{:S(2)}) collective-permute-start(bf16[40,128]{1,0:T(8,128)(2,1)S(1)} %get-tuple-element.26), channel_id=1, source_target_pairs={{0,6},{1,7},{2,4},{3,5},{4,2},{5,3},{6,0},{7,1},{8,14},{9,15},{10,... | collective-permute-start | bytes 30728 | tf_op jit(solution)/shard_map/ppermute | solution.py:249
  13.6 1.2 %collective-permute-start.5 = (bf16[34,128]{1,0:T(8,128)(2,1)S(1)}, bf16[34,128]{1,0:T(8,128)(2,1)S(1)}, u32[]{:S(2)}, u32[]{:S(2)}) collective-permute-start(bf16[34,128]{1,0:T(8,128)(2,1)S(1)} %get-tuple-element.25), channel_id=1, source_target_pairs={{0,4},{1,5},{2,6},{3,7},{4,0},{5,1},{6,2},{7,3},{8,12},{9,13},{10,... | collective-permute-start | bytes 26120 | tf_op jit(solution)/shard_map/ppermute | solution.py:249

commit v5 on v4

--- a/solution.py
+++ b/solution.py
@@ -57,7 +57,7 @@
 
 
 def terms_kernel(sub_count, regions, count_ref, place_ref, infl_ref, level_ref, innov_ref, error_ref, obs_ref,
-                 terms_ref, weights_ref, far_ref, far_later_ref, rows_ref, error32, innov32):
+                 terms_ref, weights_ref, far_ref, rows_ref, error32, innov32):
     blocks, members, per_block = obs_ref.shape
     here, near, far = neighbours(regions)
     sub_here = lax.axis_index("sub")
@@ -99,7 +99,6 @@
             terms_ref[first + i, 0:HALF, :] = jnp.where(from_top, top, bottom)
             terms_ref[first + i, HALF:USED, :] = jnp.where(row8 % 2 == 0, weight, corner)
     write_sums(weights_ref, terms_ref, sub_count // 2, sub_count // 2, far_ref)
-    write_sums(weights_ref, terms_ref, 0, sub_count // 2, far_later_ref)
 
 
 def write_sums(weights_ref, terms_ref, first, count, out_ref):
@@ -118,10 +117,14 @@
         for i in range(group - 1):
             extra = jnp.where(pair == i, totals[i][HALF:], extra)
         extras.append(extra)
+    rest = out_ref.shape[0] - sum_rows(count, 8)
+    if rest > 0:
+        extras.append(jnp.zeros((rest, 128), jnp.float32))
     out_ref[...] = jnp.concatenate(matrices + extras, axis=0)[: out_ref.shape[0]].astype(out_ref.dtype)
 
 
-def near_kernel(sub_count, terms_ref, weights_ref, near_ref):
+def near_kernel(sub_count, terms_ref, weights_ref, near_ref, far_later_ref):
+    write_sums(weights_ref, terms_ref, 0, sub_count // 2, far_later_ref)
     write_sums(weights_ref, terms_ref, sub_count + sub_count // 2, sub_count // 2, near_ref)
 
 
@@ -223,16 +226,15 @@
         cost_estimate=HEAD_COST,
     )()
     obs_count, place = lax.optimization_barrier((obs_count, place))
-    terms, weights, far, far_later = pl.pallas_call(
+    terms, weights, far = pl.pallas_call(
         functools.partial(terms_kernel, sub_count, regions),
         out_shape=(
             jax.ShapeDtypeStruct((blocks, USED, 128), jnp.float32),
             jax.ShapeDtypeStruct((3 * sub_count, blocks, 128), jnp.float32),
             sums(wide),
-            sums(wide),
         ),
         in_specs=[pl.BlockSpec(memory_space=pltpu.SMEM)] + [vmem] * 6,
-        out_specs=(vmem,) * 4,
+        out_specs=(vmem,) * 3,
         scratch_shapes=[
             pltpu.VMEM((8, 128), jnp.float32),
             pltpu.VMEM((blocks, 128), jnp.float32),
@@ -255,19 +257,19 @@
         return (r + 2 * (r % 2) - 1) % regions
 
     from_far = moved(far, across)
-    from_far_later = moved(far_later, lambda r: sibling(across(r)))
-    near = pl.pallas_call(
+    near, far_later = pl.pallas_call(
         functools.partial(near_kernel, sub_count),
-        out_shape=sums(narrow),
+        out_shape=(sums(narrow), sums(wide)),
         in_specs=[vmem] * 2,
-        out_specs=vmem,
+        out_specs=(vmem, vmem),
         compiler_params=params,
         cost_estimate=pl.CostEstimate(flops=blocks * wide * 256, bytes_accessed=blocks * USED * 512, transcendentals=0),
     )(terms, weights)
     from_near = moved(near, sibling)
+    from_far_later = moved(far_later, lambda r: sibling(across(r)))
     here, beside, later = pl.pallas_call(
         functools.partial(rest_kernel, sub_count),
-        out_shape=(sums(wide, jnp.float32), sums(narrow), sums(wide, jnp.float32)),
+        out_shape=(sums(wide, jnp.float32), sums(wide + 8), sums(wide, jnp.float32)),
         in_specs=[vmem] * 2,
         out_specs=(vmem,) * 3,
         compiler_params=params,

time: 16.2 us -> 16.2 us (level)
  starting transfers between devices: 10.1 us -> 9.69 us
  waiting for transfers between devices: 2.24 us -> 2.64 us
    ppermute x7, starting transfers between devices: 10.1 us -> 9.69 us  [moved(): lax.ppermute(x, AXES, [(index[r, s], index[region_to(r), s ^ step]) for r...]
    ppermute x7, waiting for transfers between devices: 2.24 us -> 2.64 us  [moved(): lax.ppermute(x, AXES, [(index[r, s], index[region_to(r), s ^ step]) for r...]
  transfers between devices with their start and end apart: 7 -> 7, of which waited for: 5 -> 4; matrix products, arithmetic and copies ran while one was open for 0% -> 0% of each run, Pallas kernels for 2% -> 3%
where the time goes in v5:
time: 16.2 us; the launch traced here: 16 us
  starting transfers between devices  9.69 us (60%)
  waiting for transfers between devices  2.64 us (16%)
  Pallas kernels  1.99 us (12%)
  between operations  1.48 us (9%)
  local copies, waits for them, and re-layouts  0.21 us (1%)
    ppermute x7, starting transfers between devices, moved(): lax.ppermute(x, AXES, [(index[r, s], index[region_to(r), s ^ step]) for r...  9.69 us
    ppermute x7, waiting for transfers between devices, moved(): lax.ppermute(x, AXES, [(index[r, s], index[region_to(r), s ^ step]) for r...  2.64 us
    pallas_call x1, Pallas kernels, local(): pl.pallas_call(project_kernel, out_shape=(jax.ShapeDtypeStruct((2, cells)...  1.09 us
    pallas_call x1, Pallas kernels, local(): pl.pallas_call(functools.partial(terms_kernel, sub_count, regions), out_s...  0.46 us
  transfers between devices with their start and end apart: 7, of which 4 were waited for; matrix products, arithmetic and copies ran while one was open for 0% of the time, Pallas kernels for 3%

profile of v5, /device:TPU:0, one launch (start us, length us, event | category | flops | bytes accessed | tf_op | source)
XLA Modules:
  0.0 16.0 jit_solution(15058423085691617526)
XLA Ops:
  0.6 0.0 copy-start.3
  0.6 0.0 copy-start.2
  0.7 0.0 copy-start.1
  0.7 0.0 copy-start.4
  0.7 0.0 copy-start.5
  0.7 0.0 copy-start
  1.5 0.0 copy-done.3
  1.5 0.0 copy-done.2
  1.5 0.2 %copy-done.1 = bf16[24,64,128]{2,1,0:T(8,128)(2,1)S(1)} copy-done((bf16[24,64,128]{2,1,0:T(8,128)(2,1)S(1)}, bf16[24,64,128]{2,1,0:T(8,128)(2,1)}, u32[]{:S(2)}) %copy-start.1) | copy-done | bytes 393240
  1.7 0.0 copy-done.4
  1.7 0.0 copy-done.5
  1.7 0.5 %shard_map.87 = (f32[24,40,128]{2,1,0:T(8,128)S(1)}, f32[12,24,128]{2,1,0:T(8,128)S(1)}, bf16[72,128]{1,0:T(8,128)(2,1)S(1)}) custom-call(s32[1]{0:T(128)S(6)} %copy.9.count_ref, s32[1,128]{1,0:T(1,128)S(1)} %shard_map.86.place_ref, s32[4,24]{1,0:T(4,128)S(1)} %bitcast.4, s32[4,24]{1,0:T(4,128)S(1)} %bitcast.5, bf16[24,128]{1,0:T(8,128)(2,1)S(1)} %copy-done.2, ...), custom_call_target="tpu_custom_call" | custom-call | flops 125829120 | bytes 393216 | tf_op jit(solution)/shard_map/pallas_call | solution.py:229
  2.1 3.4 %collective-permute-start.2 = (bf16[72,128]{1,0:T(8,128)(2,1)S(1)}, bf16[72,128]{1,0:T(8,128)(2,1)S(1)}, u32[]{:S(2)}, u32[]{:S(2)}) collective-permute-start(bf16[72,128]{1,0:T(8,128)(2,1)S(1)} %get-tuple-element.24), channel_id=1, source_target_pairs={{0,28},{1,29},{2,30},{3,31},{4,8},{5,9},{6,10},{7,11},{8,4},{9,5},... | collective-permute-start | bytes 55304 | tf_op jit(solution)/shard_map/ppermute | solution.py:251
  5.5 0.2 %shard_map.89 = (bf16[68,128]{1,0:T(8,128)(2,1)S(1)}, bf16[72,128]{1,0:T(8,128)(2,1)S(1)}) custom-call(f32[24,40,128]{2,1,0:T(8,128)S(1)} %get-tuple-element.18.terms_ref, f32[12,24,128]{2,1,0:T(8,128)S(1)} %get-tuple-element.19.weights_ref), custom_call_target="tpu_custom_call" | custom-call | flops 442368 | bytes 491520 | tf_op jit(solution)/shard_map/pallas_call | solution.py:260
  5.7 0.1 collective-permute-start.1
  5.8 0.2 %shard_map.88 = (f32[72,128]{1,0:T(8,128)S(1)}, bf16[80,128]{1,0:T(8,128)(2,1)S(1)}, f32[72,128]{1,0:T(8,128)S(1)}) custom-call(f32[24,40,128]{2,1,0:T(8,128)S(1)} %get-tuple-element.18.terms_ref, f32[12,24,128]{2,1,0:T(8,128)S(1)} %get-tuple-element.19.weights_ref), custom_call_target="tpu_custom_call" | custom-call | flops 1327104 | bytes 491520 | tf_op jit(solution)/shard_map/pallas_call | solution.py:270
  6.0 0.6 %collective-permute-start = (bf16[80,128]{1,0:T(8,128)(2,1)S(1)}, bf16[80,128]{1,0:T(8,128)(2,1)S(1)}, u32[]{:S(2)}, u32[]{:S(2)}) collective-permute-start(bf16[80,128]{1,0:T(8,128)(2,1)S(1)} %get-tuple-element.20), channel_id=1, source_target_pairs={{0,4},{1,5},{2,6},{3,7},{4,0},{5,1},{6,2},{7,3},{8,12},{9,13},{10,... | collective-permute-start | bytes 61448 | tf_op jit(solution)/shard_map/ppermute | solution.py:251
  6.6 0.6 %collective-permute-start.4 = (bf16[72,128]{1,0:T(8,128)(2,1)S(1)}, bf16[72,128]{1,0:T(8,128)(2,1)S(1)}, u32[]{:S(2)}, u32[]{:S(2)}) collective-permute-start(bf16[72,128]{1,0:T(8,128)(2,1)S(1)} %get-tuple-element.26), channel_id=1, source_target_pairs={{0,24},{1,25},{2,26},{3,27},{4,12},{5,13},{6,14},{7,15},{8,0},{9,1... | collective-permute-start | bytes 55304 | tf_op jit(solution)/shard_map/ppermute | solution.py:251
  7.2 0.0 collective-permute-done.1.refs_0_
  7.2 0.0 collective-permute-done.2.refs_2_
  7.2 1.6 %collective-permute-start.3 = (bf16[72,128]{1,0:T(8,128)(2,1)S(1)}, bf16[72,128]{1,0:T(8,128)(2,1)S(1)}, u32[]{:S(2)}, u32[]{:S(2)}) collective-permute-start(bf16[72,128]{1,0:T(8,128)(2,1)S(1)} %shard_map.90), channel_id=1, source_target_pairs={{0,5},{1,4},{2,7},{3,6},{4,1},{5,0},{6,3},{7,2},{8,13},{9,12},{10,... | collective-permute-start | bytes 55304 | tf_op jit(solution)/shard_map/ppermute | solution.py:251
  8.8 1.6 %collective-permute-done.4.refs_3_ = bf16[72,128]{1,0:T(8,128)(2,1)S(1)} collective-permute-done((bf16[72,128]{1,0:T(8,128)(2,1)S(1)}, bf16[72,128]{1,0:T(8,128)(2,1)S(1)}, u32[]{:S(2)}, u32[]{:S(2)}) %collective-permute-start.4) | collective-permute-done | bytes 18464 | tf_op jit(solution)/shard_map/ppermute | solution.py:251
  10.3 0.0 collective-permute-done.refs_0_
  10.4 0.1 collective-permute-done.3.refs_1_
  10.5 3.1 %collective-permute-start.6 = (bf16[40,128]{1,0:T(8,128)(2,1)S(1)}, bf16[40,128]{1,0:T(8,128)(2,1)S(1)}, u32[]{:S(2)}, u32[]{:S(2)}) collective-permute-start(bf16[40,128]{1,0:T(8,128)(2,1)S(1)} %get-tuple-element.28), channel_id=1, source_target_pairs={{0,6},{1,7},{2,4},{3,5},{4,2},{5,3},{6,0},{7,1},{8,14},{9,15},{10,... | collective-permute-start | bytes 30728 | tf_op jit(solution)/shard_map/ppermute | solution.py:251
  13.5 0.4 %collective-permute-start.5 = (bf16[34,128]{1,0:T(8,128)(2,1)S(1)}, bf16[34,128]{1,0:T(8,128)(2,1)S(1)}, u32[]{:S(2)}, u32[]{:S(2)}) collective-permute-start(bf16[34,128]{1,0:T(8,128)(2,1)S(1)} %get-tuple-element.27), channel_id=1, source_target_pairs={{0,4},{1,5},{2,6},{3,7},{4,0},{5,1},{6,2},{7,3},{8,12},{9,13},{10,... | collective-permute-start | bytes 26120 | tf_op jit(solution)/shard_map/ppermute | solution.py:251
  13.9 0.8 %collective-permute-done.5.kept_ref = bf16[34,128]{1,0:T(8,128)(2,1)S(1)} collective-permute-done((bf16[34,128]{1,0:T(8,128)(2,1)S(1)}, bf16[34,128]{1,0:T(8,128)(2,1)S(1)}, u32[]{:S(2)}, u32[]{:S(2)}) %collective-permute-start.5) | collective-permute-done | bytes 8736 | tf_op jit(solution)/shard_map/ppermute | solution.py:251
  14.8 0.2 collective-permute-done.6.got_ref
  14.9 0.0 copy-done
  14.9 1.1 %shard_map.92 = (f32[2,4096]{1,0:T(2,128)}, f32[2,4096]{1,0:T(2,128)}) custom-call(bf16[34,128]{1,0:T(8,128)(2,1)S(1)} %collective-permute-done.5.kept_ref, bf16[40,128]{1,0:T(8,128)(2,1)S(1)} %collective-permute-done.6.got_ref, bf16[128,4096]{1,0:T(8,128)(2,1)S(1)} %bitcast.3), custom_call_target="tpu_custom_call" | custom-call | flops 150994944 | bytes 1048576 | tf_op jit(solution)/shard_map/pallas_call | solution.py:303
  (3 shorter events, 0.0 us)
Async XLA Ops:
  0.6 0.8 %copy-start.3 = (bf16[24,128]{1,0:T(8,128)(2,1)S(1)}, bf16[24,128]{1,0:T(8,128)(2,1)}, u32[]{:S(2)}) copy-start(bf16[24,128]{1,0:T(8,128)(2,1)} %error_ref.1) | copy-start | bytes 18436
  0.6 0.8 %copy-start.2 = (bf16[24,128]{1,0:T(8,128)(2,1)S(1)}, bf16[24,128]{1,0:T(8,128)(2,1)}, u32[]{:S(2)}) copy-start(bf16[24,128]{1,0:T(8,128)(2,1)} %innov_ref.1) | copy-start | bytes 18436
  0.7 1.0 %copy-start.1 = (bf16[24,64,128]{2,1,0:T(8,128)(2,1)S(1)}, bf16[24,64,128]{2,1,0:T(8,128)(2,1)}, u32[]{:S(2)}) copy-start(bf16[24,64,128]{2,1,0:T(8,128)(2,1)} %obs_ref.1) | copy-start | bytes 1179652
  0.7 1.0 %copy-start.4 = (s32[24,4]{0,1:T(4,128)S(1)}, s32[24,4]{0,1:T(4,128)}, u32[]{:S(2)}) copy-start(s32[24,4]{0,1:T(4,128)} %param.11) | copy-start | bytes 1156
  0.7 1.0 %copy-start.5 = (s32[24,4]{0,1:T(4,128)S(1)}, s32[24,4]{0,1:T(4,128)}, u32[]{:S(2)}) copy-start(s32[24,4]{0,1:T(4,128)} %param.12) | copy-start | bytes 1156
  0.7 14.2 %copy-start = (bf16[2,64,4096]{2,1,0:T(8,128)(2,1)S(1)}, bf16[2,64,4096]{2,1,0:T(8,128)(2,1)}, u32[]{:S(2)}) copy-start(bf16[2,64,4096]{2,1,0:T(8,128)(2,1)} %param.7) | copy-start | bytes 3145732
  2.1 5.0 %collective-permute-start.2 = (bf16[72,128]{1,0:T(8,128)(2,1)S(1)}, bf16[72,128]{1,0:T(8,128)(2,1)S(1)}, u32[]{:S(2)}, u32[]{:S(2)}) collective-permute-start(bf16[72,128]{1,0:T(8,128)(2,1)S(1)} %get-tuple-element.24), channel_id=1, source_target_pairs={{0,28},{1,29},{2,30},{3,31},{4,8},{5,9},{6,10},{7,11},{8,4},{9,5},... | collective-permute-start | bytes 55304 | tf_op jit(solution)/shard_map/ppermute | solution.py:251
  5.7 1.5 %collective-permute-start.1 = (bf16[68,128]{1,0:T(8,128)(2,1)S(1)}, bf16[68,128]{1,0:T(8,128)(2,1)S(1)}, u32[]{:S(2)}, u32[]{:S(2)}) collective-permute-start(bf16[68,128]{1,0:T(8,128)(2,1)S(1)} %get-tuple-element.21), channel_id=1, source_target_pairs={{0,4},{1,5},{2,6},{3,7},{4,0},{5,1},{6,2},{7,3},{8,12},{9,13},{10,... | collective-permute-start | bytes 52232 | tf_op jit(solution)/shard_map/ppermute | solution.py:251
  6.0 4.3 %collective-permute-start = (bf16[80,128]{1,0:T(8,128)(2,1)S(1)}, bf16[80,128]{1,0:T(8,128)(2,1)S(1)}, u32[]{:S(2)}, u32[]{:S(2)}) collective-permute-start(bf16[80,128]{1,0:T(8,128)(2,1)S(1)} %get-tuple-element.20), channel_id=1, source_target_pairs={{0,4},{1,5},{2,6},{3,7},{4,0},{5,1},{6,2},{7,3},{8,12},{9,13},{10,... | collective-permute-start | bytes 61448 | tf_op jit(solution)/shard_map/ppermute | solution.py:251
  6.6 3.8 %collective-permute-start.4 = (bf16[72,128]{1,0:T(8,128)(2,1)S(1)}, bf16[72,128]{1,0:T(8,128)(2,1)S(1)}, u32[]{:S(2)}, u32[]{:S(2)}) collective-permute-start(bf16[72,128]{1,0:T(8,128)(2,1)S(1)} %get-tuple-element.26), channel_id=1, source_target_pairs={{0,24},{1,25},{2,26},{3,27},{4,12},{5,13},{6,14},{7,15},{8,0},{9,1... | collective-permute-start | bytes 55304 | tf_op jit(solution)/shard_map/ppermute | solution.py:251
  7.2 3.3 %collective-permute-start.3 = (bf16[72,128]{1,0:T(8,128)(2,1)S(1)}, bf16[72,128]{1,0:T(8,128)(2,1)S(1)}, u32[]{:S(2)}, u32[]{:S(2)}) collective-permute-start(bf16[72,128]{1,0:T(8,128)(2,1)S(1)} %shard_map.90), channel_id=1, source_target_pairs={{0,5},{1,4},{2,7},{3,6},{4,1},{5,0},{6,3},{7,2},{8,13},{9,12},{10,... | collective-permute-start | bytes 55304 | tf_op jit(solution)/shard_map/ppermute | solution.py:251
  10.5 4.5 %collective-permute-start.6 = (bf16[40,128]{1,0:T(8,128)(2,1)S(1)}, bf16[40,128]{1,0:T(8,128)(2,1)S(1)}, u32[]{:S(2)}, u32[]{:S(2)}) collective-permute-start(bf16[40,128]{1,0:T(8,128)(2,1)S(1)} %get-tuple-element.28), channel_id=1, source_target_pairs={{0,6},{1,7},{2,4},{3,5},{4,2},{5,3},{6,0},{7,1},{8,14},{9,15},{10,... | collective-permute-start | bytes 30728 | tf_op jit(solution)/shard_map/ppermute | solution.py:251
  13.5 1.2 %collective-permute-start.5 = (bf16[34,128]{1,0:T(8,128)(2,1)S(1)}, bf16[34,128]{1,0:T(8,128)(2,1)S(1)}, u32[]{:S(2)}, u32[]{:S(2)}) collective-permute-start(bf16[34,128]{1,0:T(8,128)(2,1)S(1)} %get-tuple-element.27), channel_id=1, source_target_pairs={{0,4},{1,5},{2,6},{3,7},{4,0},{5,1},{6,2},{7,3},{8,12},{9,13},{10,... | collective-permute-start | bytes 26120 | tf_op jit(solution)/shard_map/ppermute | solution.py:251

commit v6 on v5

--- a/solution.py
+++ b/solution.py
@@ -182,7 +182,8 @@
     bottom = jnp.where(place > 0, 2.0 * matrix, jnp.where((place == 0) & ~even, extra[1:2], 0.0))
     row16, lane16, _, _ = lane_patterns(16)
     weights = jnp.broadcast_to(extra[0:1], (16, 128))
-    weights = jnp.where(row16 == lane16 // 64, weights, 0.0)
+    near = weights.astype(jnp.bfloat16).astype(jnp.float32)
+    weights = jnp.where(row16 == lane16 // 64, near, jnp.where(row16 == lane16 // 64 + 2, weights - near, 0.0))
     mixer = jnp.concatenate(
         [
             jnp.where(first, top, 0.0),
@@ -198,7 +199,7 @@
         state = state_ref[:, at : at + width]
         projected = jnp.dot(mixer, state, preferred_element_type=jnp.float32)
         product = state.astype(jnp.float32) * projected[:128]
-        increment_ref[:, at : at + width] = projected[128:130]
+        increment_ref[:, at : at + width] = projected[128:130] + projected[130:132]
         drop_ref[0:1, at : at + width] = jnp.sum(product[:64], axis=0, keepdims=True)
         drop_ref[1:2, at : at + width] = jnp.sum(product[64:], axis=0, keepdims=True)
 

time: 16.2 us -> 16.2 us (level)
  no operation moved by 1% of the time
where the time goes in v6:
time: 16.2 us; the launch traced here: 16 us
  starting transfers between devices  9.69 us (60%)
  waiting for transfers between devices  2.64 us (16%)
  Pallas kernels  1.99 us (12%)
  between operations  1.48 us (9%)
  local copies, waits for them, and re-layouts  0.21 us (1%)
    ppermute x7, starting transfers between devices, moved(): lax.ppermute(x, AXES, [(index[r, s], index[region_to(r), s ^ step]) for r...  9.69 us
    ppermute x7, waiting for transfers between devices, moved(): lax.ppermute(x, AXES, [(index[r, s], index[region_to(r), s ^ step]) for r...  2.64 us
    pallas_call x1, Pallas kernels, local(): pl.pallas_call(project_kernel, out_shape=(jax.ShapeDtypeStruct((2, cells)...  1.09 us
    pallas_call x1, Pallas kernels, local(): pl.pallas_call(functools.partial(terms_kernel, sub_count, regions), out_s...  0.46 us
  transfers between devices with their start and end apart: 7, of which 4 were waited for; matrix products, arithmetic and copies ran while one was open for 0% of the time, Pallas kernels for 3%

profile of v6, /device:TPU:0, one launch (start us, length us, event | category | flops | bytes accessed | tf_op | source)
XLA Modules:
  0.0 16.0 jit_solution(6439674322025680938)
XLA Ops:
  0.6 0.0 copy-start.3
  0.6 0.0 copy-start.2
  0.7 0.0 copy-start.1
  0.7 0.0 copy-start.4
  0.7 0.0 copy-start.5
  0.7 0.0 copy-start
  1.5 0.0 copy-done.3
  1.5 0.0 copy-done.2
  1.5 0.2 %copy-done.1 = bf16[24,64,128]{2,1,0:T(8,128)(2,1)S(1)} copy-done((bf16[24,64,128]{2,1,0:T(8,128)(2,1)S(1)}, bf16[24,64,128]{2,1,0:T(8,128)(2,1)}, u32[]{:S(2)}) %copy-start.1) | copy-done | bytes 393240
  1.7 0.0 copy-done.4
  1.7 0.0 copy-done.5
  1.7 0.5 %shard_map.87 = (f32[24,40,128]{2,1,0:T(8,128)S(1)}, f32[12,24,128]{2,1,0:T(8,128)S(1)}, bf16[72,128]{1,0:T(8,128)(2,1)S(1)}) custom-call(s32[1]{0:T(128)S(6)} %copy.9.count_ref, s32[1,128]{1,0:T(1,128)S(1)} %shard_map.86.place_ref, s32[4,24]{1,0:T(4,128)S(1)} %bitcast.4, s32[4,24]{1,0:T(4,128)S(1)} %bitcast.5, bf16[24,128]{1,0:T(8,128)(2,1)S(1)} %copy-done.2, ...), custom_call_target="tpu_custom_call" | custom-call | flops 125829120 | bytes 393216 | tf_op jit(solution)/shard_map/pallas_call | solution.py:230
  2.1 3.4 %collective-permute-start.2 = (bf16[72,128]{1,0:T(8,128)(2,1)S(1)}, bf16[72,128]{1,0:T(8,128)(2,1)S(1)}, u32[]{:S(2)}, u32[]{:S(2)}) collective-permute-start(bf16[72,128]{1,0:T(8,128)(2,1)S(1)} %get-tuple-element.24), channel_id=1, source_target_pairs={{0,28},{1,29},{2,30},{3,31},{4,8},{5,9},{6,10},{7,11},{8,4},{9,5},... | collective-permute-start | bytes 55304 | tf_op jit(solution)/shard_map/ppermute | solution.py:252
  5.5 0.2 %shard_map.89 = (bf16[68,128]{1,0:T(8,128)(2,1)S(1)}, bf16[72,128]{1,0:T(8,128)(2,1)S(1)}) custom-call(f32[24,40,128]{2,1,0:T(8,128)S(1)} %get-tuple-element.18.terms_ref, f32[12,24,128]{2,1,0:T(8,128)S(1)} %get-tuple-element.19.weights_ref), custom_call_target="tpu_custom_call" | custom-call | flops 442368 | bytes 491520 | tf_op jit(solution)/shard_map/pallas_call | solution.py:261
  5.7 0.1 collective-permute-start.1
  5.8 0.2 %shard_map.88 = (f32[72,128]{1,0:T(8,128)S(1)}, bf16[80,128]{1,0:T(8,128)(2,1)S(1)}, f32[72,128]{1,0:T(8,128)S(1)}) custom-call(f32[24,40,128]{2,1,0:T(8,128)S(1)} %get-tuple-element.18.terms_ref, f32[12,24,128]{2,1,0:T(8,128)S(1)} %get-tuple-element.19.weights_ref), custom_call_target="tpu_custom_call" | custom-call | flops 1327104 | bytes 491520 | tf_op jit(solution)/shard_map/pallas_call | solution.py:271
  6.0 0.6 %collective-permute-start = (bf16[80,128]{1,0:T(8,128)(2,1)S(1)}, bf16[80,128]{1,0:T(8,128)(2,1)S(1)}, u32[]{:S(2)}, u32[]{:S(2)}) collective-permute-start(bf16[80,128]{1,0:T(8,128)(2,1)S(1)} %get-tuple-element.20), channel_id=1, source_target_pairs={{0,4},{1,5},{2,6},{3,7},{4,0},{5,1},{6,2},{7,3},{8,12},{9,13},{10,... | collective-permute-start | bytes 61448 | tf_op jit(solution)/shard_map/ppermute | solution.py:252
  6.6 0.6 %collective-permute-start.4 = (bf16[72,128]{1,0:T(8,128)(2,1)S(1)}, bf16[72,128]{1,0:T(8,128)(2,1)S(1)}, u32[]{:S(2)}, u32[]{:S(2)}) collective-permute-start(bf16[72,128]{1,0:T(8,128)(2,1)S(1)} %get-tuple-element.26), channel_id=1, source_target_pairs={{0,24},{1,25},{2,26},{3,27},{4,12},{5,13},{6,14},{7,15},{8,0},{9,1... | collective-permute-start | bytes 55304 | tf_op jit(solution)/shard_map/ppermute | solution.py:252
  7.2 0.0 collective-permute-done.1.refs_0_
  7.2 0.0 collective-permute-done.2.refs_2_
  7.2 1.6 %collective-permute-start.3 = (bf16[72,128]{1,0:T(8,128)(2,1)S(1)}, bf16[72,128]{1,0:T(8,128)(2,1)S(1)}, u32[]{:S(2)}, u32[]{:S(2)}) collective-permute-start(bf16[72,128]{1,0:T(8,128)(2,1)S(1)} %shard_map.90), channel_id=1, source_target_pairs={{0,5},{1,4},{2,7},{3,6},{4,1},{5,0},{6,3},{7,2},{8,13},{9,12},{10,... | collective-permute-start | bytes 55304 | tf_op jit(solution)/shard_map/ppermute | solution.py:252
  8.8 1.6 %collective-permute-done.4.refs_3_ = bf16[72,128]{1,0:T(8,128)(2,1)S(1)} collective-permute-done((bf16[72,128]{1,0:T(8,128)(2,1)S(1)}, bf16[72,128]{1,0:T(8,128)(2,1)S(1)}, u32[]{:S(2)}, u32[]{:S(2)}) %collective-permute-start.4) | collective-permute-done | bytes 18464 | tf_op jit(solution)/shard_map/ppermute | solution.py:252
  10.3 0.0 collective-permute-done.refs_0_
  10.4 0.1 collective-permute-done.3.refs_1_
  10.5 3.1 %collective-permute-start.6 = (bf16[40,128]{1,0:T(8,128)(2,1)S(1)}, bf16[40,128]{1,0:T(8,128)(2,1)S(1)}, u32[]{:S(2)}, u32[]{:S(2)}) collective-permute-start(bf16[40,128]{1,0:T(8,128)(2,1)S(1)} %get-tuple-element.28), channel_id=1, source_target_pairs={{0,6},{1,7},{2,4},{3,5},{4,2},{5,3},{6,0},{7,1},{8,14},{9,15},{10,... | collective-permute-start | bytes 30728 | tf_op jit(solution)/shard_map/ppermute | solution.py:252
  13.5 0.4 %collective-permute-start.5 = (bf16[34,128]{1,0:T(8,128)(2,1)S(1)}, bf16[34,128]{1,0:T(8,128)(2,1)S(1)}, u32[]{:S(2)}, u32[]{:S(2)}) collective-permute-start(bf16[34,128]{1,0:T(8,128)(2,1)S(1)} %get-tuple-element.27), channel_id=1, source_target_pairs={{0,4},{1,5},{2,6},{3,7},{4,0},{5,1},{6,2},{7,3},{8,12},{9,13},{10,... | collective-permute-start | bytes 26120 | tf_op jit(solution)/shard_map/ppermute | solution.py:252
  13.9 0.8 %collective-permute-done.5.kept_ref = bf16[34,128]{1,0:T(8,128)(2,1)S(1)} collective-permute-done((bf16[34,128]{1,0:T(8,128)(2,1)S(1)}, bf16[34,128]{1,0:T(8,128)(2,1)S(1)}, u32[]{:S(2)}, u32[]{:S(2)}) %collective-permute-start.5) | collective-permute-done | bytes 8736 | tf_op jit(solution)/shard_map/ppermute | solution.py:252
  14.8 0.2 collective-permute-done.6.got_ref
  14.9 0.0 copy-done
  14.9 1.1 %shard_map.92 = (f32[2,4096]{1,0:T(2,128)}, f32[2,4096]{1,0:T(2,128)}) custom-call(bf16[34,128]{1,0:T(8,128)(2,1)S(1)} %collective-permute-done.5.kept_ref, bf16[40,128]{1,0:T(8,128)(2,1)S(1)} %collective-permute-done.6.got_ref, bf16[128,4096]{1,0:T(8,128)(2,1)S(1)} %bitcast.3), custom_call_target="tpu_custom_call" | custom-call | flops 150994944 | bytes 1048576 | tf_op jit(solution)/shard_map/pallas_call | solution.py:304
  (3 shorter events, 0.0 us)
Async XLA Ops:
  0.6 0.8 %copy-start.3 = (bf16[24,128]{1,0:T(8,128)(2,1)S(1)}, bf16[24,128]{1,0:T(8,128)(2,1)}, u32[]{:S(2)}) copy-start(bf16[24,128]{1,0:T(8,128)(2,1)} %error_ref.1) | copy-start | bytes 18436
  0.6 0.8 %copy-start.2 = (bf16[24,128]{1,0:T(8,128)(2,1)S(1)}, bf16[24,128]{1,0:T(8,128)(2,1)}, u32[]{:S(2)}) copy-start(bf16[24,128]{1,0:T(8,128)(2,1)} %innov_ref.1) | copy-start | bytes 18436
  0.7 1.0 %copy-start.1 = (bf16[24,64,128]{2,1,0:T(8,128)(2,1)S(1)}, bf16[24,64,128]{2,1,0:T(8,128)(2,1)}, u32[]{:S(2)}) copy-start(bf16[24,64,128]{2,1,0:T(8,128)(2,1)} %obs_ref.1) | copy-start | bytes 1179652
  0.7 1.0 %copy-start.4 = (s32[24,4]{0,1:T(4,128)S(1)}, s32[24,4]{0,1:T(4,128)}, u32[]{:S(2)}) copy-start(s32[24,4]{0,1:T(4,128)} %param.11) | copy-start | bytes 1156
  0.7 1.0 %copy-start.5 = (s32[24,4]{0,1:T(4,128)S(1)}, s32[24,4]{0,1:T(4,128)}, u32[]{:S(2)}) copy-start(s32[24,4]{0,1:T(4,128)} %param.12) | copy-start | bytes 1156
  0.7 14.2 %copy-start = (bf16[2,64,4096]{2,1,0:T(8,128)(2,1)S(1)}, bf16[2,64,4096]{2,1,0:T(8,128)(2,1)}, u32[]{:S(2)}) copy-start(bf16[2,64,4096]{2,1,0:T(8,128)(2,1)} %param.7) | copy-start | bytes 3145732
  2.1 5.0 %collective-permute-start.2 = (bf16[72,128]{1,0:T(8,128)(2,1)S(1)}, bf16[72,128]{1,0:T(8,128)(2,1)S(1)}, u32[]{:S(2)}, u32[]{:S(2)}) collective-permute-start(bf16[72,128]{1,0:T(8,128)(2,1)S(1)} %get-tuple-element.24), channel_id=1, source_target_pairs={{0,28},{1,29},{2,30},{3,31},{4,8},{5,9},{6,10},{7,11},{8,4},{9,5},... | collective-permute-start | bytes 55304 | tf_op jit(solution)/shard_map/ppermute | solution.py:252
  5.7 1.5 %collective-permute-start.1 = (bf16[68,128]{1,0:T(8,128)(2,1)S(1)}, bf16[68,128]{1,0:T(8,128)(2,1)S(1)}, u32[]{:S(2)}, u32[]{:S(2)}) collective-permute-start(bf16[68,128]{1,0:T(8,128)(2,1)S(1)} %get-tuple-element.21), channel_id=1, source_target_pairs={{0,4},{1,5},{2,6},{3,7},{4,0},{5,1},{6,2},{7,3},{8,12},{9,13},{10,... | collective-permute-start | bytes 52232 | tf_op jit(solution)/shard_map/ppermute | solution.py:252
  6.0 4.3 %collective-permute-start = (bf16[80,128]{1,0:T(8,128)(2,1)S(1)}, bf16[80,128]{1,0:T(8,128)(2,1)S(1)}, u32[]{:S(2)}, u32[]{:S(2)}) collective-permute-start(bf16[80,128]{1,0:T(8,128)(2,1)S(1)} %get-tuple-element.20), channel_id=1, source_target_pairs={{0,4},{1,5},{2,6},{3,7},{4,0},{5,1},{6,2},{7,3},{8,12},{9,13},{10,... | collective-permute-start | bytes 61448 | tf_op jit(solution)/shard_map/ppermute | solution.py:252
  6.6 3.8 %collective-permute-start.4 = (bf16[72,128]{1,0:T(8,128)(2,1)S(1)}, bf16[72,128]{1,0:T(8,128)(2,1)S(1)}, u32[]{:S(2)}, u32[]{:S(2)}) collective-permute-start(bf16[72,128]{1,0:T(8,128)(2,1)S(1)} %get-tuple-element.26), channel_id=1, source_target_pairs={{0,24},{1,25},{2,26},{3,27},{4,12},{5,13},{6,14},{7,15},{8,0},{9,1... | collective-permute-start | bytes 55304 | tf_op jit(solution)/shard_map/ppermute | solution.py:252
  7.2 3.3 %collective-permute-start.3 = (bf16[72,128]{1,0:T(8,128)(2,1)S(1)}, bf16[72,128]{1,0:T(8,128)(2,1)S(1)}, u32[]{:S(2)}, u32[]{:S(2)}) collective-permute-start(bf16[72,128]{1,0:T(8,128)(2,1)S(1)} %shard_map.90), channel_id=1, source_target_pairs={{0,5},{1,4},{2,7},{3,6},{4,1},{5,0},{6,3},{7,2},{8,13},{9,12},{10,... | collective-permute-start | bytes 55304 | tf_op jit(solution)/shard_map/ppermute | solution.py:252
  10.5 4.5 %collective-permute-start.6 = (bf16[40,128]{1,0:T(8,128)(2,1)S(1)}, bf16[40,128]{1,0:T(8,128)(2,1)S(1)}, u32[]{:S(2)}, u32[]{:S(2)}) collective-permute-start(bf16[40,128]{1,0:T(8,128)(2,1)S(1)} %get-tuple-element.28), channel_id=1, source_target_pairs={{0,6},{1,7},{2,4},{3,5},{4,2},{5,3},{6,0},{7,1},{8,14},{9,15},{10,... | collective-permute-start | bytes 30728 | tf_op jit(solution)/shard_map/ppermute | solution.py:252
  13.5 1.2 %collective-permute-start.5 = (bf16[34,128]{1,0:T(8,128)(2,1)S(1)}, bf16[34,128]{1,0:T(8,128)(2,1)S(1)}, u32[]{:S(2)}, u32[]{:S(2)}) collective-permute-start(bf16[34,128]{1,0:T(8,128)(2,1)S(1)} %get-tuple-element.27), channel_id=1, source_target_pairs={{0,4},{1,5},{2,6},{3,7},{4,0},{5,1},{6,2},{7,3},{8,12},{9,13},{10,... | collective-permute-start | bytes 26120 | tf_op jit(solution)/shard_map/ppermute | solution.py:252
